TPU v7x, 512 devices: a whole 4x8x8 slice. The times are simulated.
512 devices in a mesh: seq: 128 (over x_hi, z, y), ch: 4 (over x_lo, core).
Axes of the slice: x: 4 (x_hi: 2, x_lo: 2; x = x_hi * 2 + x_lo), y: 8, z: 8, core: 2. Of those that a mesh axis runs over, the one named last changes fastest.
Arguments:
- tokens: int32 [65536], P('seq'), may hold values from 0 to 3
- hidden: bfloat16 [65536, 1024], P('seq', 'ch'), may hold values from -6 to 6
- embedding: bfloat16 [4, 1024], P(None, 'ch'), may hold values from -6 to 6
- w_in: bfloat16 [1024, 1024], P(None, 'ch'), may hold values from -0.1875 to 0.1875
- w_gate: bfloat16 [1024, 1024], P(None, 'ch'), may hold values from -0.1875 to 0.1875
- conv_w: float32 [3, 4, 1024], P(None, None, 'ch'), may hold values from -3 to 3
- channel_order: int32 [1024], replicated, may hold values from 0 to 1023, each once
- gain: float32 [1024], replicated, may hold values from 0.5 to 1.5
- w_out: bfloat16 [1024, 1024], P(None, 'ch'), may hold values from -0.1875 to 0.1875
- cotangent: bfloat16 [65536, 1024], P('seq', 'ch'), may hold values from -6 to 6
Outputs:
- output: bfloat16 [65536, 1024], P('seq', 'ch')
- grad_in: bfloat16 [1024, 1024], P(None, 'ch')
- grad_gate: bfloat16 [1024, 1024], P(None, 'ch')
- grad_out: bfloat16 [1024, 1024], P(None, 'ch')
- grad_conv: float32 [3, 4, 1024], P(None, None, 'ch')
Inputs may be any that keep to these rules, and one draw needn't show every extreme that they name: `channel_order`: each channel index once.
All inputs are finite; a program needn't handle non-finite values.
Results may differ from a plain program's by a relative error of at most 0.025.
Values may be sent and summed in bfloat16 or wider, within the bound.
A program may use at most 64 MiB of HBM per device.

v0:
```python
import jax
import jax.numpy as jnp
from jax import lax
from jax.sharding import PartitionSpec as P

DILATIONS = (1, 8, 64)
EPSILON = 1e-06


def extended(cells, sides, width):
    for axis, dim in sides:
        count = lax.axis_size(axis)
        ends = count - 1
        head = lax.slice_in_dim(cells, 0, width, axis=dim)
        tail = lax.slice_in_dim(cells, cells.shape[dim] - width, cells.shape[dim], axis=dim)
        cells = jnp.concatenate(
            [
                lax.ppermute(tail, axis, [(i, (i + 1) % count) for i in range(ends)]),
                cells,
                lax.ppermute(head, axis, [((i + 1) % count, i) for i in range(ends)]),
            ],
            axis=dim,
        )
    return cells


def partner(block, axis, bit):
    count = lax.axis_size(axis)
    route = []
    for low in range(count):
        high = low | 1 << bit
        if high != low and high < count:
            route += [(low, high), (high, low)]
    return lax.ppermute(block, axis, route)


def conv_apply(padded, weights, dilation, rows):
    total = jnp.zeros((rows, padded.shape[1]), jnp.float32)
    for position in range(4):
        begin = 2 * dilation + (position - 2) * dilation
        total = total + weights[position][None, :] * padded[begin : begin + rows].astype(
            jnp.float32
        )
    return total


def conv_transpose(padded_grad, weights, dilation, rows):
    total = jnp.zeros((rows, padded_grad.shape[1]), jnp.float32)
    for position in range(4):
        begin = 2 * dilation - (position - 2) * dilation
        total = total + weights[position][None, :] * padded_grad[begin : begin + rows].astype(
            jnp.float32
        )
    return total


def conv_weight_grad(upstream, padded_source, dilation, rows):
    upstream_wide = upstream.astype(jnp.float32)
    weight_rows = []
    for position in range(4):
        start = 2 * dilation + (position - 2) * dilation
        weight_rows.append(
            jnp.sum(upstream_wide * padded_source[start : start + rows].astype(jnp.float32), axis=0)
        )
    return jnp.stack(weight_rows)


def local(tokens, hidden, embedding, w_in, w_gate, conv_w, channel_order, gain, w_out, cotangent):
    rows = hidden.shape[0]
    width_local = hidden.shape[1]
    width_full = gain.shape[0]
    start_col = lax.axis_index("ch") * width_local
    seq_bits = lax.axis_size("seq").bit_length() - 1
    one_hot = (tokens[:, None] == jnp.arange(4, dtype=jnp.int32)[None, :]).astype(jnp.bfloat16)
    embed_rows = jnp.dot(one_hot, embedding, preferred_element_type=jnp.float32)
    local_input = (hidden.astype(jnp.float32) + embed_rows).astype(jnp.bfloat16)
    full_input = lax.all_gather(local_input, "ch", axis=1, tiled=True)
    projected = jnp.dot(full_input, w_in, preferred_element_type=jnp.float32).astype(jnp.bfloat16)
    gate_pre = jnp.dot(full_input, w_gate, preferred_element_type=jnp.float32)
    saved = []
    current = projected
    for level in range(3):
        dilation = DILATIONS[level]
        padded = extended(current, (("seq", 0),), 2 * dilation)
        saved.append(padded)
        current = conv_apply(padded, conv_w[level], dilation, rows).astype(jnp.bfloat16)
    gate_act = jax.nn.silu(gate_pre)
    gated = (current.astype(jnp.float32) * gate_act).astype(jnp.bfloat16)
    gated_full = lax.all_gather(gated, "ch", axis=1, tiled=True)
    mirrored = gated_full
    for bit_number in range(seq_bits):
        mirrored = partner(mirrored, "seq", bit_number)
    mirror_full = mirrored[::-1]
    combined = gated_full.astype(jnp.float32) + jnp.take(mirror_full, channel_order, axis=1).astype(
        jnp.float32
    )
    inv_scale = lax.rsqrt(jnp.mean(combined * combined, axis=1, keepdims=True) + EPSILON)
    normalized = (combined * inv_scale * gain[None, :]).astype(jnp.bfloat16)
    output = (
        local_input.astype(jnp.float32)
        + jnp.dot(normalized, w_out, preferred_element_type=jnp.float32)
    ).astype(jnp.bfloat16)
    grad_terms = lax.dot_general(
        cotangent, w_out, (((1,), (1,)), ((), ())), preferred_element_type=jnp.float32
    )
    grad_norm = lax.psum_scatter(
        grad_terms.astype(jnp.bfloat16), "ch", scatter_dimension=1, tiled=True
    ).astype(jnp.float32)
    own_hat = lax.dynamic_slice_in_dim(combined, start_col, width_local, 1) * inv_scale
    own_gain = lax.dynamic_slice_in_dim(gain, start_col, width_local, 0)
    scaled = grad_norm * own_gain[None, :]
    row_total = lax.psum(jnp.sum(scaled * own_hat, axis=1, keepdims=True), "ch")
    grad_comb = (inv_scale * (scaled - own_hat * row_total / width_full)).astype(jnp.bfloat16)
    grad_full = lax.all_gather(grad_comb, "ch", axis=1, tiled=True)
    inverse = (
        jnp.zeros_like(channel_order).at[channel_order].set(jnp.arange(width_full, dtype=jnp.int32))
    )
    own_inverse = lax.dynamic_slice_in_dim(inverse, start_col, width_local, 0)
    grad_mirror = jnp.take(grad_full, own_inverse, axis=1)
    for bit_number in range(seq_bits):
        grad_mirror = partner(grad_mirror, "seq", bit_number)
    grad_gated = grad_comb.astype(jnp.float32) + grad_mirror[::-1].astype(jnp.float32)
    upstream = (grad_gated * gate_act).astype(jnp.bfloat16)
    sigmoid_gate = jax.nn.sigmoid(gate_pre)
    grad_gate_pre = (
        grad_gated
        * current.astype(jnp.float32)
        * sigmoid_gate
        * (1.0 + gate_pre * (1.0 - sigmoid_gate))
    ).astype(jnp.bfloat16)
    tap_grads = [None, None, None]
    for level in (2, 1, 0):
        dilation = DILATIONS[level]
        padded_grad = extended(upstream, (("seq", 0),), 2 * dilation)
        tap_grads[level] = conv_weight_grad(upstream, saved[level], dilation, rows)
        upstream = conv_transpose(padded_grad, conv_w[level], dilation, rows).astype(jnp.bfloat16)
    contract_rows = (((0,), (0,)), ((), ()))
    local_in = lax.dot_general(
        full_input, upstream, contract_rows, preferred_element_type=jnp.float32
    )
    local_gate = lax.dot_general(
        full_input, grad_gate_pre, contract_rows, preferred_element_type=jnp.float32
    )
    local_out = lax.dot_general(
        normalized, cotangent, contract_rows, preferred_element_type=jnp.float32
    )
    summed = lax.psum((local_in, local_gate, local_out, jnp.stack(tap_grads)), "seq")
    return (
        output,
        summed[0].astype(jnp.bfloat16),
        summed[1].astype(jnp.bfloat16),
        summed[2].astype(jnp.bfloat16),
        summed[3],
    )


def solution(mesh):
    placed = (
        P("seq"),
        P("seq", "ch"),
        P(None, "ch"),
        P(None, "ch"),
        P(None, "ch"),
        P(None, None, "ch"),
        P(),
        P(),
        P(None, "ch"),
        P("seq", "ch"),
    )
    return jax.shard_map(
        local,
        mesh=mesh,
        in_specs=placed,
        out_specs=(
            P("seq", "ch"),
            P(None, "ch"),
            P(None, "ch"),
            P(None, "ch"),
            P(None, None, "ch"),
        ),
        check_vma=False,
    )
```

profile of v0, /device:TPU:6, one launch (start us, length us, event | category | flops | bytes accessed | tf_op | source)
XLA Modules:
  0.0 1346.7 jit_solution(11607735566059029526)
XLA Ops:
  9.4 32.2 %all-gather.4.cloned.1.call-done = bf16[512,1024]{1,0:T(8,128)(2,1)} async-done(((bf16[512,256]{1,0:T(8,128)(2,1)}), bf16[512,1024]{1,0:T(8,128)(2,1)}) %all-gather.4.cloned.1.call-update) | async-done | bytes 1048592 | tf_op jit(solution)/shard_map/all_gather | solution.py:77
  43.4 9.0 collective-permute-start.1
  54.6 9.1 collective-permute-done
  83.5 7.7 collective-permute-done.4
  92.9 16.9 %all-gather.6.cloned.1.call-done = bf16[512,1024]{1,0:T(8,128)(2,1)} async-done(((bf16[512,256]{1,0:T(8,128)(2,1)}), bf16[512,1024]{1,0:T(8,128)(2,1)}) %all-gather.6.cloned.1.call-update) | async-done | bytes 1048592 | tf_op jit(solution)/shard_map/all_gather | solution.py:89
  113.2 24.1 %collective-permute-done.6 = bf16[512,1024]{1,0:T(8,128)(2,1)S(1)} collective-permute-done((bf16[512,1024]{1,0:T(8,128)(2,1)}, bf16[512,1024]{1,0:T(8,128)(2,1)S(1)}, u32[]{:S(2)}, u32[]{:S(2)}) %collective-permute-start.6) | collective-permute-done | bytes 1048608 | tf_op jit(solution)/shard_map/ppermute | solution.py:34
  141.6 45.5 %collective-permute-done.7 = bf16[512,1024]{1,0:T(8,128)(2,1)S(1)} collective-permute-done((bf16[512,1024]{1,0:T(8,128)(2,1)S(1)}, bf16[512,1024]{1,0:T(8,128)(2,1)S(1)}, u32[]{:S(2)}, u32[]{:S(2)}) %collective-permute-start.7) | collective-permute-done | bytes 1048608 | tf_op jit(solution)/shard_map/ppermute | solution.py:34
  187.1 7.4 collective-permute-start.8
  194.5 46.2 %collective-permute-done.8 = bf16[512,1024]{1,0:T(8,128)(2,1)S(1)} collective-permute-done((bf16[512,1024]{1,0:T(8,128)(2,1)S(1)}, bf16[512,1024]{1,0:T(8,128)(2,1)S(1)}, u32[]{:S(2)}, u32[]{:S(2)}) %collective-permute-start.8) | collective-permute-done | bytes 1048608 | tf_op jit(solution)/shard_map/ppermute | solution.py:34
  244.3 22.3 %collective-permute-done.9 = bf16[512,1024]{1,0:T(8,128)(2,1)S(1)} collective-permute-done((bf16[512,1024]{1,0:T(8,128)(2,1)S(1)}, bf16[512,1024]{1,0:T(8,128)(2,1)S(1)}, u32[]{:S(2)}, u32[]{:S(2)}) %collective-permute-start.9) | collective-permute-done | bytes 1048608 | tf_op jit(solution)/shard_map/ppermute | solution.py:34
  271.2 43.7 %collective-permute-done.10 = bf16[512,1024]{1,0:T(8,128)(2,1)S(1)} collective-permute-done((bf16[512,1024]{1,0:T(8,128)(2,1)S(1)}, bf16[512,1024]{1,0:T(8,128)(2,1)S(1)}, u32[]{:S(2)}, u32[]{:S(2)}) %collective-permute-start.10) | collective-permute-done | bytes 1048608 | tf_op jit(solution)/shard_map/ppermute | solution.py:34
  314.9 7.9 collective-permute-start.11
  324.4 44.6 %collective-permute-done.11 = bf16[512,1024]{1,0:T(8,128)(2,1)} collective-permute-done((bf16[512,1024]{1,0:T(8,128)(2,1)S(1)}, bf16[512,1024]{1,0:T(8,128)(2,1)}, u32[]{:S(2)}, u32[]{:S(2)}) %collective-permute-start.11) | collective-permute-done | bytes 1048608 | tf_op jit(solution)/shard_map/ppermute | solution.py:34
  374.2 22.7 %collective-permute-done.12 = bf16[512,1024]{1,0:T(8,128)(2,1)S(1)} collective-permute-done((bf16[512,1024]{1,0:T(8,128)(2,1)}, bf16[512,1024]{1,0:T(8,128)(2,1)S(1)}, u32[]{:S(2)}, u32[]{:S(2)}) %collective-permute-start.12) | collective-permute-done | bytes 1048608 | tf_op jit(solution)/shard_map/ppermute | solution.py:34
  423.6 15.6 %all-gather.8.cloned.1.call-done = bf16[512,1024]{1,0:T(8,128)(2,1)} async-done(((bf16[512,256]{1,0:T(8,128)(2,1)}), bf16[512,1024]{1,0:T(8,128)(2,1)}) %all-gather.8.cloned.1.call-update) | async-done | bytes 1048592 | tf_op jit(solution)/shard_map/all_gather | solution.py:114
  462.5 11.8 collective-permute-done.14
  474.3 7.4 collective-permute-start.15
  481.7 12.1 collective-permute-done.15
  514.3 13.2 collective-permute-start.18
  551.1 12.0 collective-permute-start.20
  567.9 9.8 collective-permute-start.22
  579.4 9.9 collective-permute-start.24
  591.3 9.2 collective-permute-done.25
  602.2 738.0 %all-reduce.2 = (bf16[1024,256]{1,0:T(8,128)(2,1)}, bf16[1024,256]{1,0:T(8,128)(2,1)}, bf16[1024,256]{1,0:T(8,128)(2,1)}, f32[3,4,256]{2,1,0:T(4,128)}) all-reduce(f32[1024,256]{1,0:T(8,128)} %fusion.46, f32[1024,256]{1,0:T(8,128)S(1)} %fusion.48, f32[1024,256]{1,0:T(8,128)S(1)} %copy-done.1, ...), channel_id=1, replica_groups=mesh['seq'=128,'ch'=4] {'seq'}, use_global_device_ids=true, to_apply=%region_5.6 | all-reduce | flops 789504 | bytes 4743168 | tf_op jit(solution)/shard_map/psum | solution.py:147
  (173 shorter events, 153.7 us)
Async XLA Ops:
  7.2 34.3 %all-gather.4.cloned.1.call-start = ((), (), s32[]{:S(2)}) async-start(), calls=%async_computation.1 | async-start | bytes 1310720 | tf_op jit(solution)/shard_map/all_gather | solution.py:77
  9.3 100.5 %all-gather.6.cloned.1.call-start = ((), (), s32[]{:S(2)}) async-start(), calls=%async_computation.2 | async-start | bytes 1310720 | tf_op jit(solution)/shard_map/all_gather | solution.py:89
  43.4 11.1 collective-permute-start.1
  52.5 11.2 collective-permute-start
  65.9 11.3 collective-permute-start.2
  79.3 11.9 collective-permute-start.4
  92.8 313.3 %reduce-scatter.2.cloned.1.call-start = ((), (), s32[]{:S(2)}) async-start(), calls=%async_computation.3 | async-start | bytes 1310720 | tf_op jit(solution)/shard_map/reduce_scatter | solution.py:106
  109.8 27.5 %collective-permute-start.6 = (bf16[512,1024]{1,0:T(8,128)(2,1)}, bf16[512,1024]{1,0:T(8,128)(2,1)S(1)}, u32[]{:S(2)}, u32[]{:S(2)}) collective-permute-start(bf16[512,1024]{1,0:T(8,128)(2,1)} %all-gather.6.cloned.1.call-done), channel_id=1, source_target_pairs={{0,4},{4,0},{8,12},{12,8},{16,20},{20,16},{24,28},{28,24},{32,36},... | collective-permute-start | bytes 3145736 | tf_op jit(solution)/shard_map/ppermute | solution.py:34
  137.3 49.8 %collective-permute-start.7 = (bf16[512,1024]{1,0:T(8,128)(2,1)S(1)}, bf16[512,1024]{1,0:T(8,128)(2,1)S(1)}, u32[]{:S(2)}, u32[]{:S(2)}) collective-permute-start(bf16[512,1024]{1,0:T(8,128)(2,1)S(1)} %collective-permute-done.6), channel_id=1, source_target_pairs={{0,8},{8,0},{4,12},{12,4},{16,24},{24,16},{20,28},{28,20},{32,40},... | collective-permute-start | bytes 3145736 | tf_op jit(solution)/shard_map/ppermute | solution.py:34
  187.1 53.6 %collective-permute-start.8 = (bf16[512,1024]{1,0:T(8,128)(2,1)S(1)}, bf16[512,1024]{1,0:T(8,128)(2,1)S(1)}, u32[]{:S(2)}, u32[]{:S(2)}) collective-permute-start(bf16[512,1024]{1,0:T(8,128)(2,1)S(1)} %collective-permute-done.7), channel_id=1, source_target_pairs={{0,16},{16,0},{4,20},{20,4},{8,24},{24,8},{12,28},{28,12},{32,48},... | collective-permute-start | bytes 3145736 | tf_op jit(solution)/shard_map/ppermute | solution.py:34
  240.7 25.8 %collective-permute-start.9 = (bf16[512,1024]{1,0:T(8,128)(2,1)S(1)}, bf16[512,1024]{1,0:T(8,128)(2,1)S(1)}, u32[]{:S(2)}, u32[]{:S(2)}) collective-permute-start(bf16[512,1024]{1,0:T(8,128)(2,1)S(1)} %collective-permute-done.8), channel_id=1, source_target_pairs={{0,32},{32,0},{4,36},{36,4},{8,40},{40,8},{12,44},{44,12},{16,48},... | collective-permute-start | bytes 3145736 | tf_op jit(solution)/shard_map/ppermute | solution.py:34
  266.5 48.4 %collective-permute-start.10 = (bf16[512,1024]{1,0:T(8,128)(2,1)S(1)}, bf16[512,1024]{1,0:T(8,128)(2,1)S(1)}, u32[]{:S(2)}, u32[]{:S(2)}) collective-permute-start(bf16[512,1024]{1,0:T(8,128)(2,1)S(1)} %collective-permute-done.9), channel_id=1, source_target_pairs={{0,64},{64,0},{4,68},{68,4},{8,72},{72,8},{12,76},{76,12},{16,80},... | collective-permute-start | bytes 3145736 | tf_op jit(solution)/shard_map/ppermute | solution.py:34
  314.9 54.1 %collective-permute-start.11 = (bf16[512,1024]{1,0:T(8,128)(2,1)S(1)}, bf16[512,1024]{1,0:T(8,128)(2,1)}, u32[]{:S(2)}, u32[]{:S(2)}) collective-permute-start(bf16[512,1024]{1,0:T(8,128)(2,1)S(1)} %collective-permute-done.10), channel_id=1, source_target_pairs={{0,128},{128,0},{4,132},{132,4},{8,136},{136,8},{12,140},{140,12},... | collective-permute-start | bytes 3145736 | tf_op jit(solution)/shard_map/ppermute | solution.py:34
  324.3 114.9 %all-gather.8.cloned.1.call-start = ((), (), s32[]{:S(2)}) async-start(), calls=%async_computation.4 | async-start | bytes 1310720 | tf_op jit(solution)/shard_map/all_gather | solution.py:114
  369.0 27.9 %collective-permute-start.12 = (bf16[512,1024]{1,0:T(8,128)(2,1)}, bf16[512,1024]{1,0:T(8,128)(2,1)S(1)}, u32[]{:S(2)}, u32[]{:S(2)}) collective-permute-start(bf16[512,1024]{1,0:T(8,128)(2,1)} %collective-permute-done.11), channel_id=1, source_target_pairs={{0,256},{256,0},{4,260},{260,4},{8,264},{264,8},{12,268},{268,12},... | collective-permute-start | bytes 3145736 | tf_op jit(solution)/shard_map/ppermute | solution.py:34
  458.2 16.1 %collective-permute-start.14 = (bf16[512,256]{1,0:T(8,128)(2,1)S(1)}, bf16[512,256]{1,0:T(8,128)(2,1)S(1)}, u32[]{:S(2)}, u32[]{:S(2)}) collective-permute-start(bf16[512,256]{1,0:T(8,128)(2,1)S(1)} %collective-permute-done.13), channel_id=1, source_target_pairs={{0,8},{8,0},{4,12},{12,4},{16,24},{24,16},{20,28},{28,20},{32,40},... | collective-permute-start | bytes 786440 | tf_op jit(solution)/shard_map/ppermute | solution.py:34
  474.3 19.5 %collective-permute-start.15 = (bf16[512,256]{1,0:T(8,128)(2,1)S(1)}, bf16[512,256]{1,0:T(8,128)(2,1)S(1)}, u32[]{:S(2)}, u32[]{:S(2)}) collective-permute-start(bf16[512,256]{1,0:T(8,128)(2,1)S(1)} %collective-permute-done.14), channel_id=1, source_target_pairs={{0,16},{16,0},{4,20},{20,4},{8,24},{24,8},{12,28},{28,12},{32,48},... | collective-permute-start | bytes 786440 | tf_op jit(solution)/shard_map/ppermute | solution.py:34
  502.0 12.3 collective-permute-start.17
  514.3 17.5 %collective-permute-start.18 = (bf16[512,256]{1,0:T(8,128)(2,1)S(1)}, bf16[512,256]{1,0:T(8,128)(2,1)S(1)}, u32[]{:S(2)}, u32[]{:S(2)}) collective-permute-start(bf16[512,256]{1,0:T(8,128)(2,1)S(1)} %collective-permute-done.17), channel_id=1, source_target_pairs={{0,128},{128,0},{4,132},{132,4},{8,136},{136,8},{12,140},{140,12},... | collective-permute-start | bytes 786440 | tf_op jit(solution)/shard_map/ppermute | solution.py:34
  546.3 19.2 %collective-permute-start.21 = (bf16[128,256]{1,0:T(8,128)(2,1)S(1)}, bf16[128,256]{1,0:T(8,128)(2,1)S(1)}, u32[]{:S(2)}, u32[]{:S(2)}) collective-permute-start(bf16[128,256]{1,0:T(8,128)(2,1)S(1)} %get-tuple-element.35), channel_id=1, source_target_pairs={{0,4},{4,8},{8,12},{12,16},{16,20},{20,24},{24,28},{28,32},{32,36}... | collective-permute-start | bytes 196616 | tf_op jit(solution)/shard_map/ppermute | solution.py:18
  551.1 14.4 %collective-permute-start.20 = (bf16[128,256]{1,0:T(8,128)(2,1)S(1)}, bf16[128,256]{1,0:T(8,128)(2,1)S(1)}, u32[]{:S(2)}, u32[]{:S(2)}) collective-permute-start(bf16[128,256]{1,0:T(8,128)(2,1)S(1)} %get-tuple-element.34), channel_id=1, source_target_pairs={{4,0},{8,4},{12,8},{16,12},{20,16},{24,20},{28,24},{32,28},{36,32}... | collective-permute-start | bytes 196616 | tf_op jit(solution)/shard_map/ppermute | solution.py:20
  566.0 11.8 collective-permute-start.23
  579.4 11.9 collective-permute-start.24
  589.3 11.2 collective-permute-start.25
  (50 other events, 2184.9 us)
Sparse Core Ops, SparseCore 0:
  10.7 30.7 all-gather.3
  93.0 16.7 all-gather.5
  324.4 19.5 reduce-scatter.1
  416.2 22.8 all-gather.7
where the time goes:
time: 1350 us
  blocking collectives  744 us (55%)
  waiting for transfers between devices  399 us (30%)
  starting transfers between devices  138 us (10%)
  local copies, waits for them, and re-layouts  24.3 us (2%)
  between operations  14.7 us (1%)
  matrix products  13.6 us (1%)
    psum x1, blocking collectives, local(): lax.psum((local_in, local_gate, local_out, jnp.stack(tap_grads)), 'seq')  738 us
    ppermute x14, waiting for transfers between devices, partner(): return lax.ppermute(block, axis, route)  300 us
    ppermute x14, starting transfers between devices, partner(): return lax.ppermute(block, axis, route)  74.7 us
    ppermute x6, starting transfers between devices, extended(): lax.ppermute(head, axis, [((i + 1) % count, i) for i in range(ends)])  44.6 us
    ppermute x6, waiting for transfers between devices, extended(): lax.ppermute(tail, axis, [(i, (i + 1) % count) for i in range(ends)])  33.3 us
    all_gather x1, waiting for transfers between devices, local(): full_input = lax.all_gather(local_input, 'ch', axis=1, tiled=True)  32.2 us
  transfers between devices with their start and end apart: 30, of which 23 were waited for; matrix products, arithmetic and copies ran while one was open for 2% of the time, Pallas kernels for 0%

commit v1 on v0

--- a/solution.py
+++ b/solution.py
@@ -1,6 +1,10 @@
+import functools
+
 import jax
 import jax.numpy as jnp
 from jax import lax
+from jax.experimental import pallas as pl
+from jax.experimental.pallas import tpu as pltpu
 from jax.sharding import PartitionSpec as P
 
 DILATIONS = (1, 8, 64)
@@ -24,14 +28,9 @@
     return cells
 
 
-def partner(block, axis, bit):
+def mirror_blocks(block, axis):
     count = lax.axis_size(axis)
-    route = []
-    for low in range(count):
-        high = low | 1 << bit
-        if high != low and high < count:
-            route += [(low, high), (high, low)]
-    return lax.ppermute(block, axis, route)
+    return lax.ppermute(block, axis, [(i, count - 1 - i) for i in range(count)])
 
 
 def conv_apply(padded, weights, dilation, rows):
@@ -64,13 +63,238 @@
         )
     return jnp.stack(weight_rows)
 
+MESH = pl.DeviceIdType.MESH
+
+
+def ring_sizes(count):
+    return {128: (2, 8, 8), 8: (2, 2, 2), 4: (1, 2, 2)}[count]
+
+
+def reduce_kernel(
+    sizes,
+    g0_ref, g1_ref, g2_ref, conv_ref,
+    o0_ref, o1_ref, o2_ref, oconv_ref,
+    send1, recv1, send2, recv2, whole,
+    s1, r1, s2, r2, s3, r3, s4, r4,
+):
+    xs, zs, ys = sizes
+    seq = lax.axis_index("seq")
+    my_y = lax.rem(seq, ys)
+    my_z = lax.rem(lax.div(seq, ys), zs)
+    my_x = lax.div(seq, ys * zs)
+
+    def at(x, z, y):
+        return {"seq": (x * zs + z) * ys + y}
+
+    first = (ys, zs)
+    second = (zs, ys)
+    me1 = (my_y, my_z)
+    me2 = (my_z, my_y)
+
+    def first_peer(h, t):
+        return at(my_x, my_z, t) if h == 0 else at(my_x, t, my_y)
+
+    def second_peer(h, x, t):
+        return at(x, t, my_y) if h == 0 else at(x, my_z, t)
+
+    barrier = pltpu.get_barrier_semaphore()
+    greeted = 0
+    for h in range(2):
+        for d in range(1, first[h]):
+            pl.semaphore_signal(
+                barrier, inc=1, device_id=first_peer(h, lax.rem(me1[h] + d, first[h])), device_id_type=MESH
+            )
+            greeted += 1
+    for dx in range(1, xs):
+        x = lax.rem(my_x + dx, xs)
+        for dz in range(zs):
+            pl.semaphore_signal(barrier, inc=1, device_id=at(x, lax.rem(my_z + dz, zs), my_y), device_id_type=MESH)
+            greeted += 1
+        for dy in range(1, ys):
+            pl.semaphore_signal(barrier, inc=1, device_id=at(x, my_z, lax.rem(my_y + dy, ys)), device_id_type=MESH)
+            greeted += 1
+
+    grads = (g0_ref, g1_ref, g2_ref)
+    n = len(grads)
+    rows = g0_ref.shape[0]
+    conv_rows = conv_ref.shape[0]
+    for h in range(2):
+        lanes = slice(128 * h, 128 * h + 128)
+        size = rows // first[h]
+        for k in range(first[h]):
+            for g in range(n):
+                send1[h, k, g * size : (g + 1) * size, :] = grads[g][k * size : (k + 1) * size, lanes].astype(
+                    jnp.bfloat16
+                )
+            send1[h, k, n * size : n * size + conv_rows, :] = conv_ref[:, lanes].astype(jnp.bfloat16)
+    pl.semaphore_wait(barrier, greeted)
+
+    pending = []
+
+    def exchange1(h, slot_src, t, slot_dst):
+        return pltpu.make_async_remote_copy(
+            src_ref=send1.at[h, slot_src],
+            dst_ref=recv1.at[h, slot_dst],
+            send_sem=s1.at[h, slot_src],
+            recv_sem=r1.at[h, slot_dst],
+            device_id=first_peer(h, t),
+            device_id_type=MESH,
+        )
+
+    for d in range(1, max(first)):
+        for h in range(2):
+            t = lax.rem(me1[h] + d, first[h])
+            copy = exchange1(h, t, t, me1[h])
+            copy.start()
+            pending.append(copy)
+
+    def exchange2(h, x, t, src, dst):
+        return pltpu.make_async_remote_copy(
+            src_ref=send2.at[h, src],
+            dst_ref=recv2.at[h, dst],
+            send_sem=s2.at[h, lax.rem(my_x + x, xs) * second[h] + lax.rem(me2[h] + t, second[h])],
+            recv_sem=r2.at[h, dst],
+            device_id=second_peer(h, lax.rem(my_x + x, xs), lax.rem(me2[h] + t, second[h])),
+            device_id_type=MESH,
+        )
+
+    for h in range(2):
+        size = rows // first[h]
+        part = size // second[h]
+        total = send1[h, me1[h]].astype(jnp.float32)
+        for d in range(1, first[h]):
+            k = lax.rem(me1[h] + d, first[h])
+            exchange1(h, k, k, k).wait_recv()
+            recv = recv1[h, k].astype(jnp.float32)
+            total = total + recv
+        recv1[h, me1[h], n * size :, :] = send1[h, me1[h], n * size :, :]
+        tail = jnp.zeros((conv_rows, 128), jnp.float32)
+        for k in range(first[h]):
+            tail = tail + recv1[h, k, n * size :, :].astype(jnp.float32)
+        total = total.astype(jnp.bfloat16)
+        for k in range(second[h]):
+            for g in range(n):
+                send2[h, k, g * part : (g + 1) * part, :] = total[g * size + k * part : g * size + (k + 1) * part]
+            send2[h, k, n * part :, :] = tail.astype(jnp.bfloat16)
+        mine = my_x * second[h] + me2[h]
+        for x in range(xs):
+            for t in range(second[h]):
+                if x or t:
+                    copy = exchange2(h, x, t, lax.rem(me2[h] + t, second[h]), mine)
+                    copy.start()
+                    pending.append(copy)
+        recv2[h, mine] = send2[h, me2[h]]
+
+    def exchange3(h, t, slot):
+        place = whole.at[h, me1[h], slot]
+        return pltpu.make_async_remote_copy(
+            src_ref=place,
+            dst_ref=place,
+            send_sem=s3.at[h, t],
+            recv_sem=r3.at[h, slot],
+            device_id=second_peer(h, my_x, t),
+            device_id_type=MESH,
+        )
+
+    for h in range(2):
+        size = rows // first[h]
+        part = size // second[h]
+        for x in range(xs):
+            for t in range(second[h]):
+                if x or t:
+                    k = lax.rem(my_x + x, xs) * second[h] + lax.rem(me2[h] + t, second[h])
+                    exchange2(h, 0, 1, me2[h], k).wait_recv()
+        total = jnp.zeros((n * part + conv_rows, 128), jnp.float32)
+        for k in range(xs * second[h]):
+            total = total + recv2[h, k].astype(jnp.float32)
+        whole[h, me1[h], me2[h]] = total[: n * part].astype(jnp.bfloat16)
+        oconv_ref[:, 128 * h : 128 * h + 128] = total[n * part :]
+        for d in range(1, second[h]):
+            t = lax.rem(me2[h] + d, second[h])
+            copy = exchange3(h, t, me2[h])
+            copy.start()
+            pending.append(copy)
+
+    def exchange4(h, t, slot):
+        return pltpu.make_async_remote_copy(
+            src_ref=whole.at[h, slot],
+            dst_ref=whole.at[h, slot],
+            send_sem=s4.at[h, t],
+            recv_sem=r4.at[h, slot],
+            device_id=first_peer(h, t),
+            device_id_type=MESH,
+        )
+
+    outs = (o0_ref, o1_ref, o2_ref)
+
+    def place(h, k):
+        part = rows // first[h] // second[h]
+        size = rows // first[h]
+        for m in range(second[h]):
+            block = whole[h, k, m]
+            for g in range(n):
+                at_row = pl.multiple_of(k * size + m * part, part)
+                outs[g][pl.ds(at_row, part), 128 * h : 128 * h + 128] = block[g * part : (g + 1) * part]
+
+    for h in range(2):
+        for d in range(1, second[h]):
+            k = lax.rem(me2[h] + d, second[h])
+            exchange3(h, k, k).wait_recv()
+        for d in range(1, first[h]):
+            t = lax.rem(me1[h] + d, first[h])
+            copy = exchange4(h, t, me1[h])
+            copy.start()
+            pending.append(copy)
+    for h in range(2):
+        place(h, me1[h])
+    for d in range(1, max(first)):
+        for h in range(2):
+            k = lax.rem(me1[h] + d, first[h])
+            exchange4(h, k, k).wait_recv()
+            place(h, k)
+    for copy in pending:
+        copy.wait_send()
+
+
+def reduce_gradients(g0, g1, g2, conv):
+    sizes = ring_sizes(lax.axis_size("seq"))
+    xs, zs, ys = sizes
+    rows = g0.shape[0]
+    conv = jnp.pad(conv, ((0, 4), (0, 0)))
+    assert ys == zs
+    n = 3
+    chunk = n * rows // ys + 16
+    part = n * rows // ys // zs
+    grad = jax.ShapeDtypeStruct((rows, 256), jnp.bfloat16)
+    vmem = pl.BlockSpec(memory_space=pltpu.VMEM)
+    dma = pltpu.SemaphoreType.DMA
+    return pl.pallas_call(
+        functools.partial(reduce_kernel, sizes),
+        out_shape=(grad, grad, grad, jax.ShapeDtypeStruct(conv.shape, jnp.float32)),
+        in_specs=[vmem] * 4,
+        out_specs=(vmem,) * 4,
+        scratch_shapes=[
+            pltpu.VMEM((2, ys, chunk, 128), jnp.bfloat16),
+            pltpu.VMEM((2, ys, chunk, 128), jnp.bfloat16),
+            pltpu.VMEM((2, zs, part + 16, 128), jnp.bfloat16),
+            pltpu.VMEM((2, xs * zs, part + 16, 128), jnp.bfloat16),
+            pltpu.VMEM((2, ys, zs, part, 128), jnp.bfloat16),
+            dma((2, ys)), dma((2, ys)),
+            dma((2, xs * zs)), dma((2, xs * zs)),
+            dma((2, zs)), dma((2, zs)),
+            dma((2, ys)), dma((2, ys)),
+        ],
+        compiler_params=pltpu.CompilerParams(
+            collective_id=0, has_side_effects=True, vmem_limit_bytes=40 * 1024 * 1024
+        ),
+    )(g0, g1, g2, conv)
+
 
 def local(tokens, hidden, embedding, w_in, w_gate, conv_w, channel_order, gain, w_out, cotangent):
     rows = hidden.shape[0]
     width_local = hidden.shape[1]
     width_full = gain.shape[0]
     start_col = lax.axis_index("ch") * width_local
-    seq_bits = lax.axis_size("seq").bit_length() - 1
     one_hot = (tokens[:, None] == jnp.arange(4, dtype=jnp.int32)[None, :]).astype(jnp.bfloat16)
     embed_rows = jnp.dot(one_hot, embedding, preferred_element_type=jnp.float32)
     local_input = (hidden.astype(jnp.float32) + embed_rows).astype(jnp.bfloat16)
@@ -87,9 +311,7 @@
     gate_act = jax.nn.silu(gate_pre)
     gated = (current.astype(jnp.float32) * gate_act).astype(jnp.bfloat16)
     gated_full = lax.all_gather(gated, "ch", axis=1, tiled=True)
-    mirrored = gated_full
-    for bit_number in range(seq_bits):
-        mirrored = partner(mirrored, "seq", bit_number)
+    mirrored = lax.all_gather(mirror_blocks(gated, "seq"), "ch", axis=1, tiled=True)
     mirror_full = mirrored[::-1]
     combined = gated_full.astype(jnp.float32) + jnp.take(mirror_full, channel_order, axis=1).astype(
         jnp.float32
@@ -117,8 +339,7 @@
     )
     own_inverse = lax.dynamic_slice_in_dim(inverse, start_col, width_local, 0)
     grad_mirror = jnp.take(grad_full, own_inverse, axis=1)
-    for bit_number in range(seq_bits):
-        grad_mirror = partner(grad_mirror, "seq", bit_number)
+    grad_mirror = mirror_blocks(grad_mirror, "seq")
     grad_gated = grad_comb.astype(jnp.float32) + grad_mirror[::-1].astype(jnp.float32)
     upstream = (grad_gated * gate_act).astype(jnp.bfloat16)
     sigmoid_gate = jax.nn.sigmoid(gate_pre)
@@ -144,14 +365,10 @@
     local_out = lax.dot_general(
         normalized, cotangent, contract_rows, preferred_element_type=jnp.float32
     )
-    summed = lax.psum((local_in, local_gate, local_out, jnp.stack(tap_grads)), "seq")
-    return (
-        output,
-        summed[0].astype(jnp.bfloat16),
-        summed[1].astype(jnp.bfloat16),
-        summed[2].astype(jnp.bfloat16),
-        summed[3],
-    )
+    sum_in, sum_gate, sum_out, sum_conv = reduce_gradients(
+        local_in, local_gate, local_out, jnp.concatenate(tap_grads)
+    )
+    return output, sum_in, sum_gate, sum_out, sum_conv[:12].reshape(3, 4, width_local)
 
 
 def solution(mesh):

time: 1350 us -> 376 us (0.28)
  blocking collectives: 744 us -> 6.68 us
  waiting for transfers between devices: 399 us -> 156 us
  starting transfers between devices: 138 us -> 77.7 us
  Pallas kernels: 0 us -> 55.9 us
    psum x1 -> x0, blocking collectives: 738 us -> none  [local(): lax.psum((local_in, local_gate, local_out, jnp.stack(tap_grads)), 'seq')]
    ppermute x14 -> x2, waiting for transfers between devices: 300 us -> 18.5 us  [mirror_blocks(): return lax.ppermute(block, axis, [(i, count - 1 - i) for i in range(count)])]
    pallas_call x0 -> x1, Pallas kernels: none -> 55.9 us  [reduce_gradients(): pl.pallas_call(functools.partial(reduce_kernel, sizes), out_shape=(grad,...]
    ppermute x14 -> x2, starting transfers between devices: 74.7 us -> 19.3 us  [mirror_blocks(): return lax.ppermute(block, axis, [(i, count - 1 - i) for i in range(count)])]
    reduce_scatter x1, waiting for transfers between devices: 0.02 us -> 26.9 us  [local(): lax.psum_scatter(grad_terms.astype(jnp.bfloat16), 'ch', scatter_dimension...]
    all_gather x0 -> x1, waiting for transfers between devices: none -> 20 us  [local(): lax.all_gather(mirror_blocks(gated, 'seq'), 'ch', axis=1, tiled=True)]
  transfers between devices with their start and end apart: 30 -> 19, of which waited for: 23 -> 14; matrix products, arithmetic and copies ran while one was open for 2% -> 9% of each run, Pallas kernels for 0% -> 0%
where the time goes in v1:
time: 376 us; the launch traced here: 373 us
  waiting for transfers between devices  156 us (41%)
  starting transfers between devices  77.7 us (21%)
  Pallas kernels  55.9 us (15%)
  local copies, waits for them, and re-layouts  36.4 us (10%)
  matrix products  15.3 us (4%)
  between operations  14.7 us (4%)
  other arithmetic  10.2 us (3%)
  blocking collectives  6.68 us (2%)
    pallas_call x1, Pallas kernels, reduce_gradients(): pl.pallas_call(functools.partial(reduce_kernel, sizes), out_shape=(grad,...  55.9 us
    ppermute x6, starting transfers between devices, extended(): lax.ppermute(head, axis, [((i + 1) % count, i) for i in range(ends)])  41.8 us
    all_gather x1, waiting for transfers between devices, local(): full_input = lax.all_gather(local_input, 'ch', axis=1, tiled=True)  32.2 us
    reduce_scatter x1, waiting for transfers between devices, local(): lax.psum_scatter(grad_terms.astype(jnp.bfloat16), 'ch', scatter_dimension...  26.9 us
    all_gather x1, waiting for transfers between devices, local(): grad_full = lax.all_gather(grad_comb, 'ch', axis=1, tiled=True)  22.1 us
    ppermute x6, waiting for transfers between devices, extended(): lax.ppermute(tail, axis, [(i, (i + 1) % count) for i in range(ends)])  20.8 us
    all_gather x1, waiting for transfers between devices, local(): lax.all_gather(mirror_blocks(gated, 'seq'), 'ch', axis=1, tiled=True)  20 us
    ppermute x2, starting transfers between devices, mirror_blocks(): return lax.ppermute(block, axis, [(i, count - 1 - i) for i in range(count)])  19.3 us
  transfers between devices with their start and end apart: 19, of which 14 were waited for; matrix products, arithmetic and copies ran while one was open for 9% of the time, Pallas kernels for 0%

profile of v1, /device:TPU:6, one launch (start us, length us, event | category | flops | bytes accessed | tf_op | source)
XLA Modules:
  0.0 373.3 jit_solution(9986283116179170794)
XLA Ops:
  9.4 32.2 %all-gather.5.cloned.1.call-done = bf16[512,1024]{1,0:T(8,128)(2,1)} async-done(((bf16[512,256]{1,0:T(8,128)(2,1)}), bf16[512,1024]{1,0:T(8,128)(2,1)}) %all-gather.5.cloned.1.call-update) | async-done | bytes 1048592 | tf_op jit(solution)/shard_map/all_gather | solution.py:301
  43.4 3.4 collective-permute-start
  46.8 8.2 %collective-permute-start.1 = (bf16[2,256]{1,0:T(2,128)(2,1)S(1)}, bf16[2,256]{1,0:T(2,128)(2,1)S(1)}, u32[]{:S(2)}, u32[]{:S(2)}) collective-permute-start(bf16[2,256]{1,0:T(2,128)(2,1)S(1)} %get-tuple-element.51), channel_id=1, source_target_pairs={{4,0},{8,4},{12,8},{16,12},{20,16},{24,20},{28,24},{32,28},{36,32}... | collective-permute-start | bytes 3080 | tf_op jit(solution)/shard_map/ppermute | solution.py:24
  58.5 9.9 %collective-permute-start.3 = (bf16[16,256]{1,0:T(8,128)(2,1)S(1)}, bf16[16,256]{1,0:T(8,128)(2,1)S(1)}, u32[]{:S(2)}, u32[]{:S(2)}) collective-permute-start(bf16[16,256]{1,0:T(8,128)(2,1)S(1)} %get-tuple-element.49), channel_id=1, source_target_pairs={{4,0},{8,4},{12,8},{16,12},{20,16},{24,20},{28,24},{32,28},{36,32}... | collective-permute-start | bytes 24584 | tf_op jit(solution)/shard_map/ppermute | solution.py:24
  72.3 9.9 %collective-permute-start.5 = (bf16[128,256]{1,0:T(8,128)(2,1)S(1)}, bf16[128,256]{1,0:T(8,128)(2,1)S(1)}, u32[]{:S(2)}, u32[]{:S(2)}) collective-permute-start(bf16[128,256]{1,0:T(8,128)(2,1)S(1)} %get-tuple-element.47), channel_id=1, source_target_pairs={{4,0},{8,4},{12,8},{16,12},{20,16},{24,20},{28,24},{32,28},{36,32}... | collective-permute-start | bytes 196616 | tf_op jit(solution)/shard_map/ppermute | solution.py:24
  85.6 10.2 %collective-permute-start.6 = (bf16[512,256]{1,0:T(8,128)(2,1)S(1)}, bf16[512,256]{1,0:T(8,128)(2,1)S(1)}, u32[]{:S(2)}, u32[]{:S(2)}) collective-permute-start(bf16[512,256]{1,0:T(8,128)(2,1)S(1)} %get-tuple-element.38), channel_id=1, source_target_pairs={{0,508},{4,504},{8,500},{12,496},{16,492},{20,488},{24,484},{28,48... | collective-permute-start | bytes 786440 | tf_op jit(solution)/shard_map/ppermute | solution.py:33
  95.8 6.0 %collective-permute-done.6 = bf16[512,256]{1,0:T(8,128)(2,1)S(1)} collective-permute-done((bf16[512,256]{1,0:T(8,128)(2,1)S(1)}, bf16[512,256]{1,0:T(8,128)(2,1)S(1)}, u32[]{:S(2)}, u32[]{:S(2)}) %collective-permute-start.6) | collective-permute-done | bytes 262176 | tf_op jit(solution)/shard_map/ppermute | solution.py:33
  105.0 20.0 %all-gather.9.cloned.1.call-done = bf16[512,1024]{1,0:T(8,128)(2,1)} async-done(((bf16[512,256]{1,0:T(8,128)(2,1)}), bf16[512,1024]{1,0:T(8,128)(2,1)}) %all-gather.9.cloned.1.call-update) | async-done | bytes 1048592 | tf_op jit(solution)/shard_map/all_gather | solution.py:314
  125.1 12.6 %rev.6 = bf16[512,1024]{1,0:T(8,128)(2,1)S(1)} reverse(bf16[512,1024]{1,0:T(8,128)(2,1)} %all-gather.9.cloned.1.call-done), dimensions={0} | reverse | bytes 2097152 | tf_op jit(solution)/shard_map/rev | solution.py:315
  138.2 4.0 %gather_fusion = bf16[1024,512]{1,0:T(8,128)(2,1)S(1)} fusion(bf16[512,1024]{0,1:T(8,128)(2,1)S(1)} %copy.15, s32[1024]{0:T(1024)S(1)} %get-tuple-element.65), kind=kCustom, calls=%fused_computation | custom fusion | bytes 2101248 | tf_op jit(solution)/shard_map/jit(_take)/gather | solution.py:316
  143.5 11.2 %all-gather.7.cloned.1.call-done = bf16[512,1024]{1,0:T(8,128)(2,1)} async-done(((bf16[512,256]{1,0:T(8,128)(2,1)}), bf16[512,1024]{1,0:T(8,128)(2,1)}) %all-gather.7.cloned.1.call-update) | async-done | bytes 1048592 | tf_op jit(solution)/shard_map/all_gather | solution.py:313
  156.7 26.9 %reduce-scatter.2.cloned.1.call-done = bf16[512,256]{1,0:T(8,128)(2,1)} async-done(((bf16[512,1024]{1,0:T(8,128)(2,1)}), bf16[512,256]{1,0:T(8,128)(2,1)}) %reduce-scatter.2.cloned.1.call-update) | async-done | bytes 262160 | tf_op jit(solution)/shard_map/reduce_scatter | solution.py:328
  184.8 6.7 %psum.7 = f32[512]{0:T(512)S(1)} all-reduce(f32[512]{0:T(512)S(1)} %multiply_reduce_fusion.1), channel_id=1, replica_groups=mesh['seq'=128,'ch'=4] {'ch'}, use_global_device_ids=true, to_apply=%region_3.4 | all-reduce | flops 512 | bytes 4096 | tf_op jit(solution)/shard_map/psum | solution.py:334
  193.4 4.3 %scatter_custom_fusion = s32[1024]{0:T(1024)S(1)} fusion(s32[1024]{0:T(1024)S(1)} %get-tuple-element.64, s32[1024]{0:T(1024)S(1)} %iota.7, s32[]{:T(128)} %constant.19.clone.1), kind=kCustom, calls=%fused_computation.134 | custom fusion | bytes 4100 | tf_op jit(solution)/shard_map/scatter | solution.py:338
  198.9 22.1 %all-gather.11.cloned.1.call-done = bf16[512,1024]{1,0:T(8,128)(2,1)} async-done(((bf16[512,256]{1,0:T(8,128)(2,1)}), bf16[512,1024]{1,0:T(8,128)(2,1)}) %all-gather.11.cloned.1.call-update) | async-done | bytes 1048592 | tf_op jit(solution)/shard_map/all_gather | solution.py:336
  226.9 9.2 %collective-permute-start.7 = (bf16[512,256]{1,0:T(8,128)(2,1)S(1)}, bf16[512,256]{1,0:T(8,128)(2,1)S(1)}, u32[]{:S(2)}, u32[]{:S(2)}) collective-permute-start(bf16[512,256]{1,0:T(8,128)(2,1)S(1)} %select_bitcast_fusion), channel_id=1, source_target_pairs={{0,508},{4,504},{8,500},{12,496},{16,492},{20,488},{24,484},{28,48... | collective-permute-start | bytes 786440 | tf_op jit(solution)/shard_map/ppermute | solution.py:33
  238.2 12.4 %collective-permute-done.7 = bf16[512,256]{1,0:T(8,128)(2,1)S(1)} collective-permute-done((bf16[512,256]{1,0:T(8,128)(2,1)S(1)}, bf16[512,256]{1,0:T(8,128)(2,1)S(1)}, u32[]{:S(2)}, u32[]{:S(2)}) %collective-permute-start.7) | collective-permute-done | bytes 262176 | tf_op jit(solution)/shard_map/ppermute | solution.py:33
  253.2 9.1 %collective-permute-start.8 = (bf16[128,256]{1,0:T(8,128)(2,1)S(1)}, bf16[128,256]{1,0:T(8,128)(2,1)S(1)}, u32[]{:S(2)}, u32[]{:S(2)}) collective-permute-start(bf16[128,256]{1,0:T(8,128)(2,1)S(1)} %get-tuple-element.44), channel_id=1, source_target_pairs={{4,0},{8,4},{12,8},{16,12},{20,16},{24,20},{28,24},{32,28},{36,32}... | collective-permute-start | bytes 196616 | tf_op jit(solution)/shard_map/ppermute | solution.py:24
  267.0 7.2 %collective-permute-done.9 = bf16[128,256]{1,0:T(8,128)(2,1)S(1)} collective-permute-done((bf16[128,256]{1,0:T(8,128)(2,1)S(1)}, bf16[128,256]{1,0:T(8,128)(2,1)S(1)}, u32[]{:S(2)}, u32[]{:S(2)}) %collective-permute-start.9) | collective-permute-done | bytes 65568 | tf_op jit(solution)/shard_map/ppermute | solution.py:22
  277.1 3.3 collective-permute-start.11
  282.3 6.1 %collective-permute-done.11 = bf16[16,256]{1,0:T(8,128)(2,1)S(1)} collective-permute-done((bf16[16,256]{1,0:T(8,128)(2,1)S(1)}, bf16[16,256]{1,0:T(8,128)(2,1)S(1)}, u32[]{:S(2)}, u32[]{:S(2)}) %collective-permute-start.11) | collective-permute-done | bytes 8224 | tf_op jit(solution)/shard_map/ppermute | solution.py:22
  291.0 3.9 %collective-permute-start.13 = (bf16[2,256]{1,0:T(2,128)(2,1)S(1)}, bf16[2,256]{1,0:T(2,128)(2,1)S(1)}, u32[]{:S(2)}, u32[]{:S(2)}) collective-permute-start(bf16[2,256]{1,0:T(2,128)(2,1)S(1)} %get-tuple-element.40), channel_id=1, source_target_pairs={{0,4},{4,8},{8,12},{12,16},{16,20},{20,24},{24,28},{28,32},{32,36}... | collective-permute-start | bytes 3080 | tf_op jit(solution)/shard_map/ppermute | solution.py:22
  295.0 7.2 %collective-permute-done.13 = bf16[2,256]{1,0:T(2,128)(2,1)S(1)} collective-permute-done((bf16[2,256]{1,0:T(2,128)(2,1)S(1)}, bf16[2,256]{1,0:T(2,128)(2,1)S(1)}, u32[]{:S(2)}, u32[]{:S(2)}) %collective-permute-start.13) | collective-permute-done | bytes 1056 | tf_op jit(solution)/shard_map/ppermute | solution.py:22
  304.1 55.9 %shard_map.137 = (bf16[1024,256]{1,0:T(8,128)(2,1)S(1)}, bf16[1024,256]{1,0:T(8,128)(2,1)S(1)}, bf16[1024,256]{1,0:T(8,128)(2,1)S(1)}, f32[16,256]{1,0:T(8,128)S(1)}) custom-call(f32[1024,256]{1,0:T(8,128)S(1)} %fusion.46.g0_ref, f32[1024,256]{1,0:T(8,128)S(1)} %fusion.48.g1_ref, f32[1024,256]{1,0:T(8,128)S(1)} %fusion.62.g2_ref, f32[16,256]{1,0:T(8,128)S(1)} %pad.4.conv_ref), custom_call_target="tpu_custom_call" | custom-call | tf_op jit(solution)/shard_map/pallas_call | solution.py:271
  (175 shorter events, 56.8 us)
Async XLA Ops:
  7.2 96.2 %copy-start = (bf16[1024,256]{1,0:T(8,128)(2,1)S(1)}, bf16[1024,256]{1,0:T(8,128)(2,1)}, u32[]{:S(2)}) copy-start(bf16[1024,256]{1,0:T(8,128)(2,1)} %param.18) | copy-start | bytes 1572868
  7.2 47.8 %copy-start.17 = (f32[3,4,256]{2,1,0:T(4,128)S(1)}, f32[3,4,256]{2,1,0:T(4,128)}, u32[]{:S(2)}) copy-start(f32[3,4,256]{2,1,0:T(4,128)} %param.15) | copy-start | bytes 36868
  7.2 76.9 %copy-start.52 = (bf16[1024,256]{1,0:T(8,128)(2,1)S(1)}, bf16[1024,256]{1,0:T(8,128)(2,1)}, u32[]{:S(2)}) copy-start(bf16[1024,256]{1,0:T(8,128)(2,1)} %param.14) | copy-start | bytes 1572868
  7.2 34.3 %all-gather.5.cloned.1.call-start = ((), (), s32[]{:S(2)}) async-start(), calls=%async_computation.1 | async-start | bytes 1310720 | tf_op jit(solution)/shard_map/all_gather | solution.py:301
  9.3 115.7 %all-gather.9.cloned.1.call-start = ((), (), s32[]{:S(2)}) async-start(), calls=%async_computation.3 | async-start | bytes 1310720 | tf_op jit(solution)/shard_map/all_gather | solution.py:314
  41.5 42.6 %copy-start.50 = (bf16[512,1024]{1,0:T(8,128)(2,1)S(1)}, bf16[512,1024]{1,0:T(8,128)(2,1)}, u32[]{:S(2)}) copy-start(bf16[512,1024]{1,0:T(8,128)(2,1)} %all-gather.5.cloned.1.call-done) | copy-start | bytes 3145732
  43.4 11.7 %collective-permute-start = (bf16[2,256]{1,0:T(2,128)(2,1)S(1)}, bf16[2,256]{1,0:T(2,128)(2,1)S(1)}, u32[]{:S(2)}, u32[]{:S(2)}) collective-permute-start(bf16[2,256]{1,0:T(2,128)(2,1)S(1)} %get-tuple-element.50), channel_id=1, source_target_pairs={{0,4},{4,8},{8,12},{12,16},{16,20},{20,24},{24,28},{28,32},{32,36}... | collective-permute-start | bytes 3080 | tf_op jit(solution)/shard_map/ppermute | solution.py:22
  46.8 9.5 %collective-permute-start.1 = (bf16[2,256]{1,0:T(2,128)(2,1)S(1)}, bf16[2,256]{1,0:T(2,128)(2,1)S(1)}, u32[]{:S(2)}, u32[]{:S(2)}) collective-permute-start(bf16[2,256]{1,0:T(2,128)(2,1)S(1)} %get-tuple-element.51), channel_id=1, source_target_pairs={{4,0},{8,4},{12,8},{16,12},{20,16},{24,20},{28,24},{32,28},{36,32}... | collective-permute-start | bytes 3080 | tf_op jit(solution)/shard_map/ppermute | solution.py:24
  56.6 11.8 %collective-permute-start.2 = (bf16[16,256]{1,0:T(8,128)(2,1)S(1)}, bf16[16,256]{1,0:T(8,128)(2,1)S(1)}, u32[]{:S(2)}, u32[]{:S(2)}) collective-permute-start(bf16[16,256]{1,0:T(8,128)(2,1)S(1)} %get-tuple-element.48), channel_id=1, source_target_pairs={{0,4},{4,8},{8,12},{12,16},{16,20},{20,24},{24,28},{28,32},{32,36}... | collective-permute-start | bytes 24584 | tf_op jit(solution)/shard_map/ppermute | solution.py:22
  58.5 11.3 %collective-permute-start.3 = (bf16[16,256]{1,0:T(8,128)(2,1)S(1)}, bf16[16,256]{1,0:T(8,128)(2,1)S(1)}, u32[]{:S(2)}, u32[]{:S(2)}) collective-permute-start(bf16[16,256]{1,0:T(8,128)(2,1)S(1)} %get-tuple-element.49), channel_id=1, source_target_pairs={{4,0},{8,4},{12,8},{16,12},{20,16},{24,20},{28,24},{32,28},{36,32}... | collective-permute-start | bytes 24584 | tf_op jit(solution)/shard_map/ppermute | solution.py:24
  70.4 12.1 %collective-permute-start.4 = (bf16[128,256]{1,0:T(8,128)(2,1)S(1)}, bf16[128,256]{1,0:T(8,128)(2,1)S(1)}, u32[]{:S(2)}, u32[]{:S(2)}) collective-permute-start(bf16[128,256]{1,0:T(8,128)(2,1)S(1)} %get-tuple-element.46), channel_id=1, source_target_pairs={{0,4},{4,8},{8,12},{12,16},{16,20},{20,24},{24,28},{28,32},{32,36}... | collective-permute-start | bytes 196616 | tf_op jit(solution)/shard_map/ppermute | solution.py:22
  72.3 11.8 %collective-permute-start.5 = (bf16[128,256]{1,0:T(8,128)(2,1)S(1)}, bf16[128,256]{1,0:T(8,128)(2,1)S(1)}, u32[]{:S(2)}, u32[]{:S(2)}) collective-permute-start(bf16[128,256]{1,0:T(8,128)(2,1)S(1)} %get-tuple-element.47), channel_id=1, source_target_pairs={{4,0},{8,4},{12,8},{16,12},{20,16},{24,20},{28,24},{32,28},{36,32}... | collective-permute-start | bytes 196616 | tf_op jit(solution)/shard_map/ppermute | solution.py:24
  85.6 16.2 %collective-permute-start.6 = (bf16[512,256]{1,0:T(8,128)(2,1)S(1)}, bf16[512,256]{1,0:T(8,128)(2,1)S(1)}, u32[]{:S(2)}, u32[]{:S(2)}) collective-permute-start(bf16[512,256]{1,0:T(8,128)(2,1)S(1)} %get-tuple-element.38), channel_id=1, source_target_pairs={{0,508},{4,504},{8,500},{12,496},{16,492},{20,488},{24,484},{28,48... | collective-permute-start | bytes 786440 | tf_op jit(solution)/shard_map/ppermute | solution.py:33
  102.6 52.1 %all-gather.7.cloned.1.call-start = ((), (), s32[]{:S(2)}) async-start(), calls=%async_computation.2 | async-start | bytes 1310720 | tf_op jit(solution)/shard_map/all_gather | solution.py:313
  103.3 80.3 %reduce-scatter.2.cloned.1.call-start = ((), (), s32[]{:S(2)}) async-start(), calls=%async_computation.4 | async-start | bytes 1310720 | tf_op jit(solution)/shard_map/reduce_scatter | solution.py:328
  104.9 116.2 %all-gather.11.cloned.1.call-start = ((), (), s32[]{:S(2)}) async-start(), calls=%async_computation.5 | async-start | bytes 1310720 | tf_op jit(solution)/shard_map/all_gather | solution.py:336
  156.7 66.6 %copy-start.3 = (f32[512,1024]{1,0:T(8,128)}, f32[512,1024]{1,0:T(8,128)S(1)}, u32[]{:S(2)}) copy-start(f32[512,1024]{1,0:T(8,128)S(1)} %get-tuple-element.37) | copy-start | bytes 6291460
  226.9 23.8 %collective-permute-start.7 = (bf16[512,256]{1,0:T(8,128)(2,1)S(1)}, bf16[512,256]{1,0:T(8,128)(2,1)S(1)}, u32[]{:S(2)}, u32[]{:S(2)}) collective-permute-start(bf16[512,256]{1,0:T(8,128)(2,1)S(1)} %select_bitcast_fusion), channel_id=1, source_target_pairs={{0,508},{4,504},{8,500},{12,496},{16,492},{20,488},{24,484},{28,48... | collective-permute-start | bytes 786440 | tf_op jit(solution)/shard_map/ppermute | solution.py:33
  253.2 13.9 %collective-permute-start.8 = (bf16[128,256]{1,0:T(8,128)(2,1)S(1)}, bf16[128,256]{1,0:T(8,128)(2,1)S(1)}, u32[]{:S(2)}, u32[]{:S(2)}) collective-permute-start(bf16[128,256]{1,0:T(8,128)(2,1)S(1)} %get-tuple-element.44), channel_id=1, source_target_pairs={{4,0},{8,4},{12,8},{16,12},{20,16},{24,20},{28,24},{32,28},{36,32}... | collective-permute-start | bytes 196616 | tf_op jit(solution)/shard_map/ppermute | solution.py:24
  262.3 11.9 %collective-permute-start.9 = (bf16[128,256]{1,0:T(8,128)(2,1)S(1)}, bf16[128,256]{1,0:T(8,128)(2,1)S(1)}, u32[]{:S(2)}, u32[]{:S(2)}) collective-permute-start(bf16[128,256]{1,0:T(8,128)(2,1)S(1)} %get-tuple-element.45), channel_id=1, source_target_pairs={{0,4},{4,8},{8,12},{12,16},{16,20},{20,24},{24,28},{28,32},{32,36}... | collective-permute-start | bytes 196616 | tf_op jit(solution)/shard_map/ppermute | solution.py:22
  274.6 7.7 %collective-permute-start.10 = (bf16[16,256]{1,0:T(8,128)(2,1)S(1)}, bf16[16,256]{1,0:T(8,128)(2,1)S(1)}, u32[]{:S(2)}, u32[]{:S(2)}) collective-permute-start(bf16[16,256]{1,0:T(8,128)(2,1)S(1)} %get-tuple-element.42), channel_id=1, source_target_pairs={{4,0},{8,4},{12,8},{16,12},{20,16},{24,20},{28,24},{32,28},{36,32}... | collective-permute-start | bytes 24584 | tf_op jit(solution)/shard_map/ppermute | solution.py:24
  277.1 11.3 %collective-permute-start.11 = (bf16[16,256]{1,0:T(8,128)(2,1)S(1)}, bf16[16,256]{1,0:T(8,128)(2,1)S(1)}, u32[]{:S(2)}, u32[]{:S(2)}) collective-permute-start(bf16[16,256]{1,0:T(8,128)(2,1)S(1)} %get-tuple-element.43), channel_id=1, source_target_pairs={{0,4},{4,8},{8,12},{12,16},{16,20},{20,24},{24,28},{28,32},{32,36}... | collective-permute-start | bytes 24584 | tf_op jit(solution)/shard_map/ppermute | solution.py:22
  288.8 6.1 %collective-permute-start.12 = (bf16[2,256]{1,0:T(2,128)(2,1)S(1)}, bf16[2,256]{1,0:T(2,128)(2,1)S(1)}, u32[]{:S(2)}, u32[]{:S(2)}) collective-permute-start(bf16[2,256]{1,0:T(2,128)(2,1)S(1)} %get-tuple-element.41), channel_id=1, source_target_pairs={{4,0},{8,4},{12,8},{16,12},{20,16},{24,20},{28,24},{32,28},{36,32}... | collective-permute-start | bytes 3080 | tf_op jit(solution)/shard_map/ppermute | solution.py:24
  291.0 11.2 %collective-permute-start.13 = (bf16[2,256]{1,0:T(2,128)(2,1)S(1)}, bf16[2,256]{1,0:T(2,128)(2,1)S(1)}, u32[]{:S(2)}, u32[]{:S(2)}) collective-permute-start(bf16[2,256]{1,0:T(2,128)(2,1)S(1)} %get-tuple-element.40), channel_id=1, source_target_pairs={{0,4},{4,8},{8,12},{12,16},{16,20},{20,24},{24,28},{28,32},{32,36}... | collective-permute-start | bytes 3080 | tf_op jit(solution)/shard_map/ppermute | solution.py:22
  (49 other events, 841.0 us)
Sparse Core Ops, SparseCore 0:
  10.7 30.7 all-gather.4
  102.7 22.3 all-gather.8
  127.2 27.4 all-gather.6
  157.4 26.1 reduce-scatter.1
  193.5 27.5 all-gather.10

commit v2 on v0

v2 whole, which is shorter than its diff:
```python
import functools

import jax
import jax.numpy as jnp
from jax import lax
from jax.experimental import pallas as pl
from jax.experimental.pallas import tpu as pltpu
from jax.sharding import PartitionSpec as P

DILATIONS = (1, 8, 64)
EPSILON = 1e-06
MESH = pl.DeviceIdType.MESH
BF16 = jnp.bfloat16
F32 = jnp.float32

FWD_LEFT, FWD_RIGHT = 160, 80
BWD_LEFT, BWD_RIGHT = 80, 160
CHUNK = 64
SENDS = 160
RECEIVES = 192


def ring_sizes(count):
    return {128: (2, 8, 8), 8: (2, 2, 2), 4: (1, 2, 2)}[count]


def dot(a, b, contract):
    return lax.dot_general(a, b, ((contract[:1], contract[1:]), ((), ())), preferred_element_type=F32)


def pieces(lo, hi):
    return [(start, min(CHUNK, hi - start)) for start in range(lo, hi, CHUNK)]


def block_kernel(
    sizes, groups,
    tokens_ref, hidden_ref, embedding_ref, w_in_ref, w_gate_ref, conv_w_ref, order_ref, gain_ref, w_out_ref, cot_ref,
    output_ref, grad_in_ref, grad_gate_ref, grad_out_ref, grad_conv_ref,
    block_in, embed, level0, level1, level2, level3, gate_pre, halo_send, halo_recv, halo_late,
    gated, both, permute, cot_mix, term_send, term_recv, term_cross, norm_mix, grad_split,
    grad_gated, up3, up2, up1, product_send, product_recv, up3_low, up0_low, gate_low,
    send1, recv1, send2, recv2, whole, send_sem, recv_sem,
):
    xs, zs, ys = sizes
    count = xs * zs * ys
    rows, width = hidden_ref.shape
    full = width * groups
    eighth = rows // (2 * groups)
    half = rows // 2

    seq = lax.axis_index("seq")
    ch = lax.axis_index("ch")
    core = lax.rem(ch, 2)
    x_lo = lax.div(ch, 2)
    sibling = x_lo * 2 + 1 - core
    across = (1 - x_lo) * 2 + core
    diagonal = (1 - x_lo) * 2 + 1 - core
    mirror = count - 1 - seq
    after = lax.rem(seq + 1, count)
    before = lax.rem(seq + count - 1, count)
    my_y = lax.rem(seq, ys)
    my_z = lax.rem(lax.div(seq, ys), zs)
    my_x = lax.div(seq, ys * zs)
    left_live = (seq > 0).astype(F32)
    right_live = (seq < count - 1).astype(F32)

    def at(x, z, y):
        return {"seq": (x * zs + z) * ys + y}

    first = (ys, zs)
    second = (zs, ys)
    me1 = (my_y, my_z)
    me2 = (my_z, my_y)

    def first_peer(h, t):
        return at(my_x, my_z, t) if h == 0 else at(my_x, t, my_y)

    def second_peer(h, x, t):
        return at(x, t, my_y) if h == 0 else at(x, my_z, t)

    def top(q):
        return pl.ds(pl.multiple_of(q * eighth, eighth), eighth)

    def bottom(q):
        return pl.ds(pl.multiple_of(rows - eighth - q * eighth, eighth), eighth)

    barrier = pltpu.get_barrier_semaphore()
    greeted = []

    def greet(device):
        pl.semaphore_signal(barrier, inc=1, device_id=device, device_id_type=MESH)
        greeted.append(0)

    greet({"ch": sibling})
    greet({"ch": across})
    greet({"ch": diagonal})
    for q in range(groups):
        greet({"seq": mirror, "ch": q})
    greet({"seq": after})
    greet({"seq": before})
    for h in range(2):
        for d in range(1, first[h]):
            greet(first_peer(h, lax.rem(me1[h] + d, first[h])))
    for dx in range(1, xs):
        x = lax.rem(my_x + dx, xs)
        for dz in range(zs):
            greet(at(x, lax.rem(my_z + dz, zs), my_y))
        for dy in range(1, ys):
            greet(at(x, my_z, lax.rem(my_y + dy, ys)))

    pending = []
    bases = {}

    def base(name, size):
        if name not in bases:
            bases[name] = sum(taken for _, taken in bases.values()), size
        return bases[name][0]

    def send(src, dst, receive, device):
        copy = pltpu.make_async_remote_copy(
            src_ref=src, dst_ref=dst, send_sem=send_sem.at[len(pending)], recv_sem=recv_sem.at[receive],
            device_id=device, device_id_type=MESH,
        )
        copy.start()
        pending.append(copy)

    def arrived(dst, receive):
        pltpu.make_async_remote_copy(
            src_ref=dst, dst_ref=dst, send_sem=send_sem.at[0], recv_sem=recv_sem.at[receive],
            device_id={"ch": sibling}, device_id_type=MESH,
        ).wait_recv()

    embed[...] = jnp.zeros_like(embed)
    embed[0:4, :] = embedding_ref[...]
    hot = (lax.broadcasted_iota(jnp.int32, (16, rows), 0) == tokens_ref[...]).astype(F32).astype(BF16)
    looked_up = dot(hot, embed[...], (0, 0))
    block_in[ch] = (hidden_ref[...].astype(F32) + looked_up).astype(BF16)
    cot_mix[0:half, :] = cot_ref[0:half, :]

    pl.semaphore_wait(barrier, len(greeted))

    parts = ((rows - FWD_LEFT, FWD_LEFT), (0, FWD_RIGHT), (FWD_RIGHT, rows - FWD_LEFT - FWD_RIGHT))
    gather = base("gather", 3 * groups)

    def gather_part(i, slot):
        return block_in.at[slot, pl.ds(parts[i][0], parts[i][1])]

    def gather_send(i, slot, target):
        send(gather_part(i, slot), gather_part(i, slot), gather + i * groups + slot, {"ch": target})

    def gather_wait(i, slot):
        arrived(gather_part(i, slot), gather + i * groups + slot)

    for i in range(3):
        gather_send(i, ch, across)
        gather_send(i, ch, sibling)
    cot_sem = base("cot", 1)
    send(cot_ref.at[pl.ds(half, half)], cot_mix.at[pl.ds(half, half)], cot_sem, {"seq": mirror})

    for start in range(0, full, 128):
        place = lax.broadcasted_iota(jnp.int32, (128, full), 0) + start
        permute[start : start + 128, :] = (place == order_ref[...]).astype(F32).astype(BF16)
    flip = (
        lax.broadcasted_iota(jnp.int32, (2 * eighth, 2 * eighth), 0)
        + lax.broadcasted_iota(jnp.int32, (2 * eighth, 2 * eighth), 1)
        == 2 * eighth - 1
    ).astype(F32).astype(BF16)

    def project(i, weights):
        start, size = parts[i]
        total = jnp.zeros((size, width), F32)
        for k in range(groups):
            total = total + dot(block_in[k, start : start + size, :], weights[k * width : (k + 1) * width, :], (1, 0))
        return total

    halo = base("halo", 2)
    for i in range(2):
        gather_wait(i, across)
        gather_send(i, across, sibling)
    for i in range(2):
        start, size = parts[i]
        gather_wait(i, sibling)
        gather_wait(i, diagonal)
        projected = project(i, w_in_ref).astype(BF16)
        level0[FWD_LEFT + start : FWD_LEFT + start + size, :] = projected.astype(F32)
        keep = pl.ds(0, FWD_LEFT) if i == 0 else pl.ds(FWD_LEFT, FWD_RIGHT)
        halo_send[keep, :] = projected
        send(halo_send.at[keep], halo_recv.at[keep], halo + i, {"seq": after if i == 0 else before})
    gather_wait(2, across)
    gather_send(2, across, sibling)
    for i in range(2):
        start, size = parts[i]
        gate_pre[start : start + size, :] = project(i, w_gate_ref)

    arrived(cot_mix.at[pl.ds(half, half)], cot_sem)
    for q in range(groups):
        low = rows - eighth - q * eighth
        for part, start in enumerate((q * eighth, low)):
            term_send[q, part * eighth : (part + 1) * eighth, :] = dot(
                cot_mix[start : start + eighth, :], w_out_ref[...], (1, 1)
            ).astype(BF16)
    term = base("term", 3)
    gather_wait(2, sibling)
    gather_wait(2, diagonal)
    for i in range(2):
        target = i * 2 + 1 - core
        send(term_send.at[target], term_recv.at[i], term + i, {"ch": sibling})
    start, size = parts[2]
    level0[FWD_LEFT + start : FWD_LEFT + start + size, :] = project(2, w_in_ref).astype(BF16).astype(F32)
    gate_pre[start : start + size, :] = project(2, w_gate_ref)

    arrived(halo_recv.at[pl.ds(0, FWD_LEFT)], halo)
    arrived(halo_recv.at[pl.ds(FWD_LEFT, FWD_RIGHT)], halo + 1)
    own = FWD_LEFT + rows
    level0[0:FWD_LEFT, :] = halo_recv[0:FWD_LEFT, :].astype(F32) * left_live
    level0[own : own + FWD_RIGHT, :] = halo_recv[FWD_LEFT : FWD_LEFT + FWD_RIGHT, :].astype(F32) * right_live

    def convolve(source, level, sign, lo, hi, live, store):
        dilation = DILATIONS[level]
        for start, size in pieces(lo, hi):
            total = jnp.zeros((size, width), F32)
            for t in range(4):
                begin = start + sign * (t - 2) * dilation
                total = total + conv_w_ref[level, t : t + 1, :] * source[begin : begin + size, :]
            if live is not None:
                total = total * live
            store(start, size, total.astype(BF16).astype(F32))

    def into(target):
        def store(start, size, value):
            target[start : start + size, :] = value
        return store

    for level, (source, target) in enumerate(((level0, level1), (level1, level2))):
        lo, hi = ((8, own + 72), (24, own + 64))[level]
        convolve(source, level, 1, lo, FWD_LEFT, left_live, into(target))
        convolve(source, level, 1, FWD_LEFT, own, None, into(target))
        convolve(source, level, 1, own, hi, right_live, into(target))

    def store_gated(start, size, value):
        start = start - FWD_LEFT
        level3[start : start + size, :] = value
        gate = gate_pre[start : start + size, :]
        gated[start : start + size, :] = (value * (gate * jax.nn.sigmoid(gate))).astype(BF16)

    convolve(level2, 2, 1, FWD_LEFT, own, None, store_gated)

    mix = base("mix", 2 * groups)
    for q in range(groups):
        send(
            gated.at[pl.ds(rows - eighth - q * eighth, eighth)], both.at[ch, pl.ds(eighth, eighth)],
            mix + groups + ch, {"seq": mirror, "ch": q},
        )
    for d in range(1, groups):
        q = lax.rem(ch + d, groups)
        send(gated.at[top(q)], both.at[ch, pl.ds(0, eighth)], mix + ch, {"ch": q})
    both[ch, 0:eighth, :] = gated[top(ch), :]

    for i in range(2):
        arrived(term_recv.at[i], term + i)
    term_send[across] = (term_send[across].astype(F32) + term_recv[1 - x_lo].astype(F32)).astype(BF16)
    send(term_send.at[across], term_cross, term + 2, {"ch": across})
    arrived(term_cross, term + 2)
    grad_norm = term_send[ch].astype(F32) + term_recv[x_lo].astype(F32) + term_cross[...].astype(F32)
    scaled = grad_norm * gain_ref[...]

    for d in range(1, groups):
        q = lax.rem(ch + d, groups)
        arrived(both.at[q, pl.ds(0, eighth)], mix + q)
    for q in range(groups):
        arrived(both.at[q, pl.ds(eighth, eighth)], mix + groups + q)

    mine = jnp.concatenate([both[q] for q in range(groups)], axis=1)
    other = dot(flip, dot(mine, permute[...], (1, 0)).astype(BF16), (1, 0))
    combined = mine.astype(F32) + other
    inv_scale = lax.rsqrt(jnp.mean(combined * combined, axis=1, keepdims=True) + EPSILON)
    hat = combined * inv_scale
    normalized = (hat * gain_ref[...]).astype(BF16)
    norm_mix[top(ch), :] = normalized[:eighth]
    norm_mix[bottom(ch), :] = normalized[eighth:]
    row_total = jnp.sum(scaled * hat, axis=1, keepdims=True)
    grad_comb = (inv_scale * (scaled - hat * (row_total * (1.0 / full)))).astype(BF16)
    turned = dot(flip, dot(grad_comb, permute[...], (1, 1)).astype(BF16), (1, 0))
    returned = (grad_comb.astype(F32) + turned).astype(BF16)
    for q in range(groups):
        grad_split[q] = returned[:, q * width : (q + 1) * width]
    back = base("back", 2 * groups)
    for q in range(groups):
        send(
            grad_split.at[q, pl.ds(eighth, eighth)], grad_gated.at[bottom(ch)],
            back + groups + ch, {"seq": mirror, "ch": q},
        )
    for d in range(1, groups):
        q = lax.rem(ch + d, groups)
        send(grad_split.at[q, pl.ds(0, eighth)], grad_gated.at[top(ch)], back + ch, {"ch": q})
    grad_gated[top(ch), :] = grad_split[ch, 0:eighth, :]

    norm = base("norm", 2 * groups)

    def norm_send(q, target):
        send(norm_mix.at[top(q)], norm_mix.at[top(q)], norm + q, {"ch": target})
        send(norm_mix.at[bottom(q)], norm_mix.at[bottom(q)], norm + groups + q, {"ch": target})

    def norm_wait(q):
        arrived(norm_mix.at[top(q)], norm + q)
        arrived(norm_mix.at[bottom(q)], norm + groups + q)

    norm_send(ch, across)
    norm_send(ch, sibling)
    norm_wait(across)
    norm_send(across, sibling)
    norm_wait(sibling)
    norm_wait(diagonal)
    product = dot(norm_mix[...], w_out_ref[...], (1, 0))
    output_ref[0:half, :] = (block_in[ch, 0:half, :].astype(F32) + product[:half]).astype(BF16)
    product_send[...] = product[half:].astype(BF16)
    product_sem = base("product", 1)
    send(product_send, product_recv, product_sem, {"seq": mirror})

    conv_rows = 16
    size = full // ys
    part = size // zs
    names = ("out", "gate", "in")

    def exchange1(name, h, k):
        g = names.index(name)
        tall = size + (conv_rows if name == "in" else 0)
        return g, pl.ds(g * size, tall), base("sum" + name, 2 * ys) + h * ys + k

    def spread(name, value):
        for h in range(2):
            for k in range(first[h]):
                g = names.index(name)
                send1[h, k, g * size : (g + 1) * size, :] = value[
                    k * size : (k + 1) * size, 128 * h : 128 * h + 128
                ].astype(BF16)
        for d in range(1, ys):
            for h in range(2):
                t = lax.rem(me1[h] + d, first[h])
                _, span, sem = exchange1(name, h, me1[h])
                send(send1.at[h, t, span], recv1.at[h, me1[h], span], sem, first_peer(h, t))

    spread("out", dot(norm_mix[...], cot_mix[...], (0, 0)))

    for d in range(1, groups):
        q = lax.rem(ch + d, groups)
        arrived(grad_gated.at[top(q)], back + q)
    for q in range(groups):
        arrived(grad_gated.at[bottom(q)], back + groups + q)
    own = BWD_LEFT + rows
    for start, tall in pieces(0, rows):
        gate = gate_pre[start : start + tall, :]
        sigmoid = jax.nn.sigmoid(gate)
        grad = grad_gated[start : start + tall, :].astype(F32)
        upstream = (grad * (gate * sigmoid)).astype(BF16)
        up3_low[start : start + tall, :] = upstream
        up3[BWD_LEFT + start : BWD_LEFT + start + tall, :] = upstream.astype(F32)
        gate_low[start : start + tall, :] = (
            grad * level3[start : start + tall, :] * sigmoid * (1.0 + gate * (1.0 - sigmoid))
        ).astype(BF16)
    halo_back = base("halo_back", 2)
    send(up3_low.at[pl.ds(0, BWD_RIGHT)], halo_late.at[pl.ds(BWD_LEFT, BWD_RIGHT)], halo_back, {"seq": before})
    send(
        up3_low.at[pl.ds(rows - BWD_LEFT, BWD_LEFT)], halo_late.at[pl.ds(0, BWD_LEFT)], halo_back + 1, {"seq": after}
    )

    def against_input(value):
        return jnp.concatenate([dot(block_in[k], value, (0, 0)) for k in range(groups)], axis=0)

    spread("gate", against_input(gate_low[...]))
    arrived(halo_late.at[pl.ds(BWD_LEFT, BWD_RIGHT)], halo_back)
    arrived(halo_late.at[pl.ds(0, BWD_LEFT)], halo_back + 1)
    up3[0:BWD_LEFT, :] = halo_late[0:BWD_LEFT, :].astype(F32) * left_live
    up3[own : own + BWD_RIGHT, :] = halo_late[BWD_LEFT : BWD_LEFT + BWD_RIGHT, :].astype(F32) * right_live

    convolve(up3, 2, -1, 64, BWD_LEFT, left_live, into(up2))
    convolve(up3, 2, -1, BWD_LEFT, own, None, into(up2))
    convolve(up3, 2, -1, own, own + 24, right_live, into(up2))
    convolve(up2, 1, -1, 72, BWD_LEFT, left_live, into(up1))
    convolve(up2, 1, -1, BWD_LEFT, own, None, into(up1))
    convolve(up2, 1, -1, own, own + 8, right_live, into(up1))

    def store_last(start, tall, value):
        up0_low[start - BWD_LEFT : start - BWD_LEFT + tall, :] = value.astype(BF16)

    convolve(up1, 0, -1, BWD_LEFT, own, None, store_last)

    taps = []
    for level, (source, upstream) in enumerate(((level0, up1), (level1, up2), (level2, up3))):
        for t in range(4):
            total = jnp.zeros((8, width), F32)
            for start, tall in pieces(0, rows):
                begin = FWD_LEFT + start + (t - 2) * DILATIONS[level]
                term_product = (
                    upstream[BWD_LEFT + start : BWD_LEFT + start + tall, :] * source[begin : begin + tall, :]
                )
                total = total + jnp.sum(term_product.reshape(tall // 8, 8, width), axis=0)
            taps.append(jnp.sum(total, axis=0, keepdims=True))
    taps = jnp.concatenate(taps + [jnp.zeros((conv_rows - 12, width), F32)], axis=0).astype(BF16)
    for h in range(2):
        for k in range(first[h]):
            send1[h, k, 3 * size : 3 * size + conv_rows, :] = taps[:, 128 * h : 128 * h + 128]
    spread("in", against_input(up0_low[...]))

    arrived(product_recv, product_sem)
    output_ref[half:rows, :] = (
        block_in[ch, half:rows, :].astype(F32) + product_recv[...].astype(F32)
    ).astype(BF16)

    over = base("over", 2 * xs * zs)
    for h in range(2):
        total = send1[h, me1[h]].astype(F32)
        for d in range(1, first[h]):
            k = lax.rem(me1[h] + d, first[h])
            for name in names:
                _, span, sem = exchange1(name, h, k)
                arrived(recv1.at[h, k, span], sem)
            total = total + recv1[h, k].astype(F32)
        recv1[h, me1[h], 3 * size :, :] = send1[h, me1[h], 3 * size :, :]
        tail = jnp.zeros((conv_rows, 128), F32)
        for k in range(first[h]):
            tail = tail + recv1[h, k, 3 * size :, :].astype(F32)
        total = total.astype(BF16)
        for k in range(second[h]):
            for g in range(3):
                send2[h, k, g * part : (g + 1) * part, :] = total[g * size + k * part : g * size + (k + 1) * part]
            send2[h, k, 3 * part :, :] = tail.astype(BF16)
        slot = my_x * second[h] + me2[h]
        for dx in range(xs):
            for dt in range(second[h]):
                if dx or dt:
                    x = lax.rem(my_x + dx, xs)
                    t = lax.rem(me2[h] + dt, second[h])
                    send(send2.at[h, t], recv2.at[h, slot], over + h * xs * zs + slot, second_peer(h, x, t))
        recv2[h, slot] = send2[h, me2[h]]

    gather2 = base("gather2", 2 * zs)
    for h in range(2):
        for dx in range(xs):
            for dt in range(second[h]):
                if dx or dt:
                    k = lax.rem(my_x + dx, xs) * second[h] + lax.rem(me2[h] + dt, second[h])
                    arrived(recv2.at[h, k], over + h * xs * zs + k)
        total = jnp.zeros((3 * part + conv_rows, 128), F32)
        for k in range(xs * second[h]):
            total = total + recv2[h, k].astype(F32)
        whole[h, me1[h], me2[h]] = total[: 3 * part].astype(BF16)
        grad_conv_ref[:, 128 * h : 128 * h + 128] = total[3 * part :]
        for d in range(1, second[h]):
            t = lax.rem(me2[h] + d, second[h])
            here = whole.at[h, me1[h], me2[h]]
            send(here, here, gather2 + h * zs + me2[h], second_peer(h, my_x, t))

    gather1 = base("gather1", 2 * ys)
    outs = (grad_out_ref, grad_gate_ref, grad_in_ref)

    def place_rows(h, k):
        for m in range(second[h]):
            block = whole[h, k, m]
            for g in range(3):
                at_row = pl.multiple_of(k * size + m * part, part)
                outs[g][pl.ds(at_row, part), 128 * h : 128 * h + 128] = block[g * part : (g + 1) * part]

    for h in range(2):
        for d in range(1, second[h]):
            k = lax.rem(me2[h] + d, second[h])
            arrived(whole.at[h, me1[h], k], gather2 + h * zs + k)
        for d in range(1, first[h]):
            t = lax.rem(me1[h] + d, first[h])
            here = whole.at[h, me1[h]]
            send(here, here, gather1 + h * ys + me1[h], first_peer(h, t))
    for h in range(2):
        place_rows(h, me1[h])
    for d in range(1, ys):
        for h in range(2):
            k = lax.rem(me1[h] + d, first[h])
            arrived(whole.at[h, k], gather1 + h * ys + k)
            place_rows(h, k)
    for copy in pending:
        copy.wait_send()


def local(tokens, hidden, embedding, w_in, w_gate, conv_w, channel_order, gain, w_out, cotangent):
    rows, width = hidden.shape
    full = gain.shape[0]
    groups = lax.axis_size("ch")
    sizes = ring_sizes(lax.axis_size("seq"))
    xs, zs, ys = sizes
    size = full // ys
    part = size // zs
    eighth = rows // (2 * groups)
    extended = rows + FWD_LEFT + FWD_RIGHT
    vmem = pl.BlockSpec(memory_space=pltpu.VMEM)
    dma = pltpu.SemaphoreType.DMA

    def held(*shape, dtype=BF16):
        return pltpu.VMEM(shape, dtype)

    weight = jax.ShapeDtypeStruct((full, width), BF16)
    output, grad_in, grad_gate, grad_out, grad_conv = pl.pallas_call(
        functools.partial(block_kernel, sizes, groups),
        out_shape=(
            jax.ShapeDtypeStruct((rows, width), BF16), weight, weight, weight, jax.ShapeDtypeStruct((16, width), F32)
        ),
        in_specs=[vmem] * 10,
        out_specs=(vmem,) * 5,
        scratch_shapes=[
            held(groups, rows, width),
            held(16, width),
            held(extended, width, dtype=F32),
            held(extended, width, dtype=F32),
            held(extended, width, dtype=F32),
            held(rows, width, dtype=F32),
            held(rows, width, dtype=F32),
            held(FWD_LEFT + FWD_RIGHT, width),
            held(FWD_LEFT + FWD_RIGHT, width),
            held(BWD_LEFT + BWD_RIGHT, width),
            held(rows, width),
            held(groups, 2 * eighth, width),
            held(full, full),
            held(rows, width),
            held(groups, 2 * eighth, full),
            held(2, 2 * eighth, full),
            held(2 * eighth, full),
            held(rows, full),
            held(groups, 2 * eighth, width),
            held(rows, width),
            held(extended, width, dtype=F32),
            held(extended, width, dtype=F32),
            held(extended, width, dtype=F32),
            held(rows // 2, width),
            held(rows // 2, width),
            held(rows, width),
            held(rows, width),
            held(rows, width),
            held(2, ys, 3 * size + 16, 128),
            held(2, ys, 3 * size + 16, 128),
            held(2, zs, 3 * part + 16, 128),
            held(2, xs * zs, 3 * part + 16, 128),
            held(2, ys, zs, 3 * part, 128),
            dma((SENDS,)),
            dma((RECEIVES,)),
        ],
        compiler_params=pltpu.CompilerParams(
            collective_id=0, has_side_effects=True, vmem_limit_bytes=56 * 1024 * 1024
        ),
    )(
        tokens.reshape(1, rows), hidden, embedding, w_in, w_gate, conv_w, channel_order.reshape(1, full),
        gain.reshape(1, full), w_out, cotangent,
    )
    return output, grad_in, grad_gate, grad_out, grad_conv[:12].reshape(3, 4, width)


def solution(mesh):
    placed = (
        P("seq"),
        P("seq", "ch"),
        P(None, "ch"),
        P(None, "ch"),
        P(None, "ch"),
        P(None, None, "ch"),
        P(),
        P(),
        P(None, "ch"),
        P("seq", "ch"),
    )
    return jax.shard_map(
        local,
        mesh=mesh,
        in_specs=placed,
        out_specs=(
            P("seq", "ch"),
            P(None, "ch"),
            P(None, "ch"),
            P(None, "ch"),
            P(None, None, "ch"),
        ),
        check_vma=False,
    )
```

time: 1350 us -> 135 us (0.10)
  the two profiles are of different devices: /device:TPU:6 before, /device:TPU:1 now
where the time goes in v2:
time: 135 us
  Pallas kernels  128 us (95%)
  local copies, waits for them, and re-layouts  6.31 us (5%)
    pallas_call x1, Pallas kernels, local(): pl.pallas_call(functools.partial(block_kernel, sizes, groups), out_shape=...  128 us
    unnamed x10, local copies, waits for them, and re-layouts  4.92 us

profile of v2, /device:TPU:1, one launch (start us, length us, event | category | flops | bytes accessed | tf_op | source)
XLA Modules:
  0.0 134.8 jit_solution(17945232313450942216)
XLA Ops:
  0.6 127.8 %shard_map.137 = (bf16[512,256]{1,0:T(8,128)(2,1)}, bf16[1024,256]{1,0:T(8,128)(2,1)}, bf16[1024,256]{1,0:T(8,128)(2,1)}, bf16[1024,256]{1,0:T(8,128)(2,1)}, f32[16,256]{1,0:T(8,128)}) custom-call(s32[1,512]{1,0:T(1,128)} %bitcast.7, bf16[512,256]{1,0:T(8,128)(2,1)} %hidden_ref.1, bf16[4,256]{1,0:T(4,128)(2,1)} %embedding_ref.1, bf16[1024,256]{1,0:T(8,128)(2,1)} %w_in_ref.1, ...), custom_call_target="tpu_custom_call" | custom-call | tf_op jit(solution)/shard_map/pallas_call | solution.py:500
  128.5 0.0 copy-start.2
  128.5 1.4 %reshape.25 = f32[3,4,256]{2,1,0:T(4,128)} reshape(f32[12,256]{1,0:T(8,128)} %bitcast.4) | data formatting | bytes 24576 | tf_op jit(solution)/shard_map/reshape | solution.py:551
  129.9 1.7 %copy.19 = bf16[512,256]{1,0:T(8,128)(2,1)} copy(bf16[512,256]{1,0:T(8,128)(2,1)} %get-tuple-element.20) | data formatting | bytes 524288
  131.5 0.0 copy-done.2
  131.5 0.0 copy-start.1
  131.5 0.8 copy.20
  132.3 0.4 copy-done.1
  132.8 0.0 copy-start
  132.8 0.8 copy.21
  133.6 0.4 copy-done
  134.0 0.8 copy.22
Async XLA Ops:
  128.5 3.1 %copy-start.2 = (bf16[1024,256]{1,0:T(8,128)(2,1)S(1)}, bf16[1024,256]{1,0:T(8,128)(2,1)}, u32[]{:S(2)}) copy-start(bf16[1024,256]{1,0:T(8,128)(2,1)} %get-tuple-element.21) | copy-start | bytes 1572868
  131.5 1.2 copy-start.1
  132.8 1.2 copy-start

commit v3 on v2

--- a/solution.py
+++ b/solution.py
@@ -16,8 +16,8 @@
 FWD_LEFT, FWD_RIGHT = 160, 80
 BWD_LEFT, BWD_RIGHT = 80, 160
 CHUNK = 64
-SENDS = 160
-RECEIVES = 192
+SENDS = 224
+RECEIVES = 256
 
 
 def ring_sizes(count):
@@ -34,12 +34,14 @@
 
 def block_kernel(
     sizes, groups,
-    tokens_ref, hidden_ref, embedding_ref, w_in_ref, w_gate_ref, conv_w_ref, order_ref, gain_ref, w_out_ref, cot_ref,
+    tokens_in, hidden_in, embedding_in, w_in_in, w_gate_in, conv_w_in, order_in, gain_in, w_out_in, cot_in,
+    output_out, grad_in_out, grad_gate_out, grad_out_out, grad_conv_out,
+    tokens_ref, hidden_ref, w_in_ref, w_gate_ref, conv_w_ref, order_ref, gain_ref, w_out_ref,
     output_ref, grad_in_ref, grad_gate_ref, grad_out_ref, grad_conv_ref,
     block_in, embed, level0, level1, level2, level3, gate_pre, halo_send, halo_recv, halo_late,
     gated, both, permute, cot_mix, term_send, term_recv, term_cross, norm_mix, grad_split,
     grad_gated, up3, up2, up1, product_send, product_recv, up3_low, up0_low, gate_low,
-    send1, recv1, send2, recv2, whole, send_sem, recv_sem,
+    send1, recv1, send2, recv2, whole, conv_x, send_sem, recv_sem, local_sem,
 ):
     xs, zs, ys = sizes
     count = xs * zs * ys
@@ -131,11 +133,33 @@
         ).wait_recv()
 
     embed[...] = jnp.zeros_like(embed)
-    embed[0:4, :] = embedding_ref[...]
+    loads = {}
+    for name, src, dst in (
+        ("tokens", tokens_in, tokens_ref),
+        ("embedding", embedding_in, embed.at[pl.ds(0, 4)]),
+        ("hidden", hidden_in, hidden_ref),
+        ("cot", cot_in.at[pl.ds(0, half)], cot_mix.at[pl.ds(0, half)]),
+        ("order", order_in, order_ref),
+        ("w_in", w_in_in, w_in_ref),
+        ("w_gate", w_gate_in, w_gate_ref),
+        ("w_out", w_out_in, w_out_ref),
+        ("conv_w", conv_w_in, conv_w_ref),
+        ("gain", gain_in, gain_ref),
+    ):
+        loads[name] = pltpu.make_async_copy(src, dst, local_sem.at[len(loads)])
+        loads[name].start()
+    stores = []
+
+    def store_out(src, dst):
+        copy = pltpu.make_async_copy(src, dst, local_sem.at[len(loads) + len(stores)])
+        copy.start()
+        stores.append(copy)
+
+    for name in ("tokens", "embedding", "hidden"):
+        loads[name].wait()
     hot = (lax.broadcasted_iota(jnp.int32, (16, rows), 0) == tokens_ref[...]).astype(F32).astype(BF16)
     looked_up = dot(hot, embed[...], (0, 0))
     block_in[ch] = (hidden_ref[...].astype(F32) + looked_up).astype(BF16)
-    cot_mix[0:half, :] = cot_ref[0:half, :]
 
     pl.semaphore_wait(barrier, len(greeted))
 
@@ -155,8 +179,9 @@
         gather_send(i, ch, across)
         gather_send(i, ch, sibling)
     cot_sem = base("cot", 1)
-    send(cot_ref.at[pl.ds(half, half)], cot_mix.at[pl.ds(half, half)], cot_sem, {"seq": mirror})
-
+    send(cot_in.at[pl.ds(half, half)], cot_mix.at[pl.ds(half, half)], cot_sem, {"seq": mirror})
+
+    loads["order"].wait()
     for start in range(0, full, 128):
         place = lax.broadcasted_iota(jnp.int32, (128, full), 0) + start
         permute[start : start + 128, :] = (place == order_ref[...]).astype(F32).astype(BF16)
@@ -173,6 +198,7 @@
             total = total + dot(block_in[k, start : start + size, :], weights[k * width : (k + 1) * width, :], (1, 0))
         return total
 
+    loads["w_in"].wait()
     halo = base("halo", 2)
     for i in range(2):
         gather_wait(i, across)
@@ -188,10 +214,13 @@
         send(halo_send.at[keep], halo_recv.at[keep], halo + i, {"seq": after if i == 0 else before})
     gather_wait(2, across)
     gather_send(2, across, sibling)
+    loads["w_gate"].wait()
     for i in range(2):
         start, size = parts[i]
         gate_pre[start : start + size, :] = project(i, w_gate_ref)
 
+    loads["w_out"].wait()
+    loads["cot"].wait()
     arrived(cot_mix.at[pl.ds(half, half)], cot_sem)
     for q in range(groups):
         low = rows - eighth - q * eighth
@@ -209,6 +238,8 @@
     level0[FWD_LEFT + start : FWD_LEFT + start + size, :] = project(2, w_in_ref).astype(BF16).astype(F32)
     gate_pre[start : start + size, :] = project(2, w_gate_ref)
 
+    loads["conv_w"].wait()
+    loads["gain"].wait()
     arrived(halo_recv.at[pl.ds(0, FWD_LEFT)], halo)
     arrived(halo_recv.at[pl.ds(FWD_LEFT, FWD_RIGHT)], halo + 1)
     own = FWD_LEFT + rows
@@ -309,38 +340,135 @@
     norm_send(ch, sibling)
     norm_wait(across)
     norm_send(across, sibling)
-    norm_wait(sibling)
-    norm_wait(diagonal)
-    product = dot(norm_mix[...], w_out_ref[...], (1, 0))
-    output_ref[0:half, :] = (block_in[ch, 0:half, :].astype(F32) + product[:half]).astype(BF16)
-    product_send[...] = product[half:].astype(BF16)
-    product_sem = base("product", 1)
-    send(product_send, product_recv, product_sem, {"seq": mirror})
 
     conv_rows = 16
     size = full // ys
     part = size // zs
     names = ("out", "gate", "in")
-
-    def exchange1(name, h, k):
+    early, late = ("out", "gate"), ("in",)
+
+    def span1(name):
+        return pl.ds(0, size + (conv_rows if name == "in" else 0))
+
+    def sem1(name, h, k):
+        return base("sum " + name, 2 * ys) + h * ys + k
+
+    def spread(name, value):
         g = names.index(name)
-        tall = size + (conv_rows if name == "in" else 0)
-        return g, pl.ds(g * size, tall), base("sum" + name, 2 * ys) + h * ys + k
-
-    def spread(name, value):
         for h in range(2):
             for k in range(first[h]):
-                g = names.index(name)
-                send1[h, k, g * size : (g + 1) * size, :] = value[
-                    k * size : (k + 1) * size, 128 * h : 128 * h + 128
-                ].astype(BF16)
+                send1[g, h, k, 0:size, :] = value[k * size : (k + 1) * size, 128 * h : 128 * h + 128].astype(BF16)
         for d in range(1, ys):
             for h in range(2):
                 t = lax.rem(me1[h] + d, first[h])
-                _, span, sem = exchange1(name, h, me1[h])
-                send(send1.at[h, t, span], recv1.at[h, me1[h], span], sem, first_peer(h, t))
-
-    spread("out", dot(norm_mix[...], cot_mix[...], (0, 0)))
+                send(
+                    send1.at[g, h, t, span1(name)], recv1.at[g, h, me1[h], span1(name)],
+                    sem1(name, h, me1[h]), first_peer(h, t),
+                )
+
+    def tall2(unit, same):
+        return len(unit) * part + (conv_rows if same and unit is late else 0)
+
+    def rows2(unit, same):
+        return pl.ds(names.index(unit[0]) * part, tall2(unit, same))
+
+    def sem2(unit, h, k):
+        return base("over " + unit[0], 2 * xs * zs) + h * xs * zs + k
+
+    def second_sum(unit):
+        for h in range(2):
+            for name in unit:
+                g = names.index(name)
+                total = send1[g, h, me1[h], 0:size, :].astype(F32)
+                for d in range(1, first[h]):
+                    k = lax.rem(me1[h] + d, first[h])
+                    arrived(recv1.at[g, h, k, span1(name)], sem1(name, h, k))
+                    total = total + recv1[g, h, k, 0:size, :].astype(F32)
+                total = total.astype(BF16)
+                for k in range(second[h]):
+                    send2[h, k, g * part : (g + 1) * part, :] = total[k * part : (k + 1) * part]
+            if unit is late:
+                recv1[2, h, me1[h], size:, :] = send1[2, h, me1[h], size:, :]
+                tail = jnp.zeros((conv_rows, 128), F32)
+                for k in range(first[h]):
+                    tail = tail + recv1[2, h, k, size:, :].astype(F32)
+                for k in range(second[h]):
+                    send2[h, k, 3 * part :, :] = tail.astype(BF16)
+            slot = my_x * second[h] + me2[h]
+            for dx in reversed(range(xs)):
+                for dt in range(second[h]):
+                    if dx or dt:
+                        x = lax.rem(my_x + dx, xs)
+                        t = lax.rem(me2[h] + dt, second[h])
+                        span = rows2(unit, dx == 0)
+                        send(send2.at[h, t, span], recv2.at[h, slot, span], sem2(unit, h, slot), second_peer(h, x, t))
+            span = rows2(unit, True)
+            recv2[h, slot, span, :] = send2[h, me2[h], span, :]
+
+    def sem3(unit, h, k):
+        return base("gather2 " + unit[0], 2 * zs) + h * zs + k
+
+    conv_sem = base("conv", 2 * xs)
+
+    def span3(unit):
+        return pl.ds(names.index(unit[0]) * part, len(unit) * part)
+
+    def second_gather(unit):
+        for h in range(2):
+            for dx in range(xs):
+                for dt in range(second[h]):
+                    if dx or dt:
+                        k = lax.rem(my_x + dx, xs) * second[h] + lax.rem(me2[h] + dt, second[h])
+                        arrived(recv2.at[h, k, rows2(unit, dx == 0)], sem2(unit, h, k))
+            total = jnp.zeros((len(unit) * part, 128), F32)
+            for k in range(xs * second[h]):
+                total = total + recv2[h, k, span3(unit), :].astype(F32)
+            whole[names.index(unit[0]) // 2, h, me1[h], me2[h], 0 : len(unit) * part] = total.astype(BF16)
+            for d in range(1, second[h]):
+                t = lax.rem(me2[h] + d, second[h])
+                here = whole.at[names.index(unit[0]) // 2, h, me1[h], me2[h], pl.ds(0, len(unit) * part)]
+                send(here, here, sem3(unit, h, me2[h]), second_peer(h, my_x, t))
+            if unit is late:
+                tail = jnp.zeros((conv_rows, 128), F32)
+                for t in range(second[h]):
+                    tail = tail + recv2[h, my_x * second[h] + t, 3 * part :, :].astype(F32)
+                conv_x[h, my_x] = tail.astype(BF16)
+                for dx in range(1, xs):
+                    here = conv_x.at[h, my_x]
+                    send(here, here, conv_sem + h * xs + my_x, at(lax.rem(my_x + dx, xs), my_z, my_y))
+
+    def sem4(unit, h, k):
+        return base("gather1 " + unit[0], 2 * ys) + h * ys + k
+
+    def block4(unit, h, k):
+        return whole.at[names.index(unit[0]) // 2, h, k, pl.ds(0, zs), pl.ds(0, len(unit) * part)]
+
+    def first_gather(unit):
+        u = names.index(unit[0]) // 2
+        for h in range(2):
+            for d in range(1, second[h]):
+                k = lax.rem(me2[h] + d, second[h])
+                arrived(whole.at[u, h, me1[h], k, pl.ds(0, len(unit) * part)], sem3(unit, h, k))
+            for d in range(1, first[h]):
+                t = lax.rem(me1[h] + d, first[h])
+                send(block4(unit, h, me1[h]), block4(unit, h, me1[h]), sem4(unit, h, me1[h]), first_peer(h, t))
+
+    outs = (grad_out_ref, grad_gate_ref, grad_in_ref)
+
+    def place_rows(unit, h, k):
+        for i, name in enumerate(unit):
+            block = whole[names.index(unit[0]) // 2, h, k, :, i * part : (i + 1) * part, :]
+            at_row = pl.multiple_of(k * size, size)
+            outs[names.index(name)][pl.ds(at_row, size), 128 * h : 128 * h + 128] = block.reshape(size, 128)
+
+    def finish(unit):
+        for h in range(2):
+            place_rows(unit, h, me1[h])
+        for d in range(1, ys):
+            for h in range(2):
+                k = lax.rem(me1[h] + d, first[h])
+                arrived(block4(unit, h, k), sem4(unit, h, k))
+                place_rows(unit, h, k)
 
     for d in range(1, groups):
         q = lax.rem(ch + d, groups)
@@ -367,7 +495,11 @@
     def against_input(value):
         return jnp.concatenate([dot(block_in[k], value, (0, 0)) for k in range(groups)], axis=0)
 
+    norm_wait(sibling)
+    norm_wait(diagonal)
+    spread("out", dot(norm_mix[...], cot_mix[...], (0, 0)))
     spread("gate", against_input(gate_low[...]))
+
     arrived(halo_late.at[pl.ds(BWD_LEFT, BWD_RIGHT)], halo_back)
     arrived(halo_late.at[pl.ds(0, BWD_LEFT)], halo_back + 1)
     up3[0:BWD_LEFT, :] = halo_late[0:BWD_LEFT, :].astype(F32) * left_live
@@ -399,85 +531,57 @@
     taps = jnp.concatenate(taps + [jnp.zeros((conv_rows - 12, width), F32)], axis=0).astype(BF16)
     for h in range(2):
         for k in range(first[h]):
-            send1[h, k, 3 * size : 3 * size + conv_rows, :] = taps[:, 128 * h : 128 * h + 128]
+            send1[2, h, k, size : size + conv_rows, :] = taps[:, 128 * h : 128 * h + 128]
     spread("in", against_input(up0_low[...]))
 
+    second_sum(early)
+
+    product = dot(norm_mix[...], w_out_ref[...], (1, 0))
+    product_send[...] = product[half:].astype(BF16)
+    product_sem = base("product", 1)
+    send(product_send, product_recv, product_sem, {"seq": mirror})
+    output_ref[0:half, :] = (block_in[ch, 0:half, :].astype(F32) + product[:half]).astype(BF16)
+    store_out(output_ref.at[pl.ds(0, half)], output_out.at[pl.ds(0, half)])
+
+    second_sum(late)
+    second_gather(early)
     arrived(product_recv, product_sem)
     output_ref[half:rows, :] = (
         block_in[ch, half:rows, :].astype(F32) + product_recv[...].astype(F32)
     ).astype(BF16)
-
-    over = base("over", 2 * xs * zs)
+    store_out(output_ref.at[pl.ds(half, half)], output_out.at[pl.ds(half, half)])
+    second_gather(late)
+    first_gather(early)
+    first_gather(late)
     for h in range(2):
-        total = send1[h, me1[h]].astype(F32)
-        for d in range(1, first[h]):
-            k = lax.rem(me1[h] + d, first[h])
-            for name in names:
-                _, span, sem = exchange1(name, h, k)
-                arrived(recv1.at[h, k, span], sem)
-            total = total + recv1[h, k].astype(F32)
-        recv1[h, me1[h], 3 * size :, :] = send1[h, me1[h], 3 * size :, :]
+        for dx in range(1, xs):
+            x = lax.rem(my_x + dx, xs)
+            arrived(conv_x.at[h, x], conv_sem + h * xs + x)
         tail = jnp.zeros((conv_rows, 128), F32)
-        for k in range(first[h]):
-            tail = tail + recv1[h, k, 3 * size :, :].astype(F32)
-        total = total.astype(BF16)
-        for k in range(second[h]):
-            for g in range(3):
-                send2[h, k, g * part : (g + 1) * part, :] = total[g * size + k * part : g * size + (k + 1) * part]
-            send2[h, k, 3 * part :, :] = tail.astype(BF16)
-        slot = my_x * second[h] + me2[h]
-        for dx in range(xs):
-            for dt in range(second[h]):
-                if dx or dt:
-                    x = lax.rem(my_x + dx, xs)
-                    t = lax.rem(me2[h] + dt, second[h])
-                    send(send2.at[h, t], recv2.at[h, slot], over + h * xs * zs + slot, second_peer(h, x, t))
-        recv2[h, slot] = send2[h, me2[h]]
-
-    gather2 = base("gather2", 2 * zs)
-    for h in range(2):
-        for dx in range(xs):
-            for dt in range(second[h]):
-                if dx or dt:
-                    k = lax.rem(my_x + dx, xs) * second[h] + lax.rem(me2[h] + dt, second[h])
-                    arrived(recv2.at[h, k], over + h * xs * zs + k)
-        total = jnp.zeros((3 * part + conv_rows, 128), F32)
-        for k in range(xs * second[h]):
-            total = total + recv2[h, k].astype(F32)
-        whole[h, me1[h], me2[h]] = total[: 3 * part].astype(BF16)
-        grad_conv_ref[:, 128 * h : 128 * h + 128] = total[3 * part :]
-        for d in range(1, second[h]):
-            t = lax.rem(me2[h] + d, second[h])
-            here = whole.at[h, me1[h], me2[h]]
-            send(here, here, gather2 + h * zs + me2[h], second_peer(h, my_x, t))
-
-    gather1 = base("gather1", 2 * ys)
-    outs = (grad_out_ref, grad_gate_ref, grad_in_ref)
-
-    def place_rows(h, k):
-        for m in range(second[h]):
-            block = whole[h, k, m]
-            for g in range(3):
-                at_row = pl.multiple_of(k * size + m * part, part)
-                outs[g][pl.ds(at_row, part), 128 * h : 128 * h + 128] = block[g * part : (g + 1) * part]
-
-    for h in range(2):
-        for d in range(1, second[h]):
-            k = lax.rem(me2[h] + d, second[h])
-            arrived(whole.at[h, me1[h], k], gather2 + h * zs + k)
-        for d in range(1, first[h]):
-            t = lax.rem(me1[h] + d, first[h])
-            here = whole.at[h, me1[h]]
-            send(here, here, gather1 + h * ys + me1[h], first_peer(h, t))
-    for h in range(2):
-        place_rows(h, me1[h])
-    for d in range(1, ys):
-        for h in range(2):
-            k = lax.rem(me1[h] + d, first[h])
-            arrived(whole.at[h, k], gather1 + h * ys + k)
-            place_rows(h, k)
+        for x in range(xs):
+            tail = tail + conv_x[h, x].astype(F32)
+        for level in range(3):
+            grad_conv_ref[level, :, 128 * h : 128 * h + 128] = tail[4 * level : 4 * level + 4]
+    store_out(grad_conv_ref, grad_conv_out)
+    finish(early)
+    store_out(grad_out_ref, grad_out_out)
+    store_out(grad_gate_ref, grad_gate_out)
+    finish(late)
+    store_out(grad_in_ref, grad_in_out)
     for copy in pending:
         copy.wait_send()
+    for copy in stores:
+        copy.wait()
+
+
+def hand_over(*refs):
+    count = len(refs) // 2
+    sems = refs[-1]
+    copies = [pltpu.make_async_copy(refs[i], refs[count + i], sems.at[i]) for i in range(count)]
+    for copy in copies:
+        copy.start()
+    for copy in copies:
+        copy.wait()
 
 
 def local(tokens, hidden, embedding, w_in, w_gate, conv_w, channel_order, gain, w_out, cotangent):
@@ -490,21 +594,35 @@
     part = size // zs
     eighth = rows // (2 * groups)
     extended = rows + FWD_LEFT + FWD_RIGHT
-    vmem = pl.BlockSpec(memory_space=pltpu.VMEM)
+    anywhere = pl.BlockSpec(memory_space=pl.ANY)
     dma = pltpu.SemaphoreType.DMA
 
     def held(*shape, dtype=BF16):
         return pltpu.VMEM(shape, dtype)
 
     weight = jax.ShapeDtypeStruct((full, width), BF16)
-    output, grad_in, grad_gate, grad_out, grad_conv = pl.pallas_call(
+    results = (
+        jax.ShapeDtypeStruct((rows, width), BF16), weight, weight, weight, jax.ShapeDtypeStruct((3, 4, width), F32)
+    )
+    computed = pl.pallas_call(
         functools.partial(block_kernel, sizes, groups),
-        out_shape=(
-            jax.ShapeDtypeStruct((rows, width), BF16), weight, weight, weight, jax.ShapeDtypeStruct((16, width), F32)
-        ),
-        in_specs=[vmem] * 10,
-        out_specs=(vmem,) * 5,
+        out_shape=results,
+        in_specs=[anywhere] * 10,
+        out_specs=(anywhere,) * 5,
         scratch_shapes=[
+            held(1, rows, dtype=jnp.int32),
+            held(rows, width),
+            held(full, width),
+            held(full, width),
+            held(3, 4, width, dtype=F32),
+            held(1, full, dtype=jnp.int32),
+            held(1, full, dtype=F32),
+            held(full, width),
+            held(rows, width),
+            held(full, width),
+            held(full, width),
+            held(full, width),
+            held(3, 4, width, dtype=F32),
             held(groups, rows, width),
             held(16, width),
             held(extended, width, dtype=F32),
@@ -533,13 +651,15 @@
             held(rows, width),
             held(rows, width),
             held(rows, width),
-            held(2, ys, 3 * size + 16, 128),
-            held(2, ys, 3 * size + 16, 128),
+            held(3, 2, ys, size + 16, 128),
+            held(3, 2, ys, size + 16, 128),
             held(2, zs, 3 * part + 16, 128),
             held(2, xs * zs, 3 * part + 16, 128),
-            held(2, ys, zs, 3 * part, 128),
+            held(2, 2, ys, zs, 2 * part, 128),
+            held(2, xs, 16, 128),
             dma((SENDS,)),
             dma((RECEIVES,)),
+            dma((16,)),
         ],
         compiler_params=pltpu.CompilerParams(
             collective_id=0, has_side_effects=True, vmem_limit_bytes=56 * 1024 * 1024
@@ -548,7 +668,14 @@
         tokens.reshape(1, rows), hidden, embedding, w_in, w_gate, conv_w, channel_order.reshape(1, full),
         gain.reshape(1, full), w_out, cotangent,
     )
-    return output, grad_in, grad_gate, grad_out, grad_conv[:12].reshape(3, 4, width)
+    return pl.pallas_call(
+        hand_over,
+        out_shape=results,
+        in_specs=[anywhere] * 5,
+        out_specs=(anywhere,) * 5,
+        scratch_shapes=[dma((5,))],
+        compiler_params=pltpu.CompilerParams(vmem_limit_bytes=60 * 1024 * 1024),
+    )(*computed)
 
 
 def solution(mesh):

time: 135 us -> 174 us (1.29)
  the two profiles are of different devices: /device:TPU:1 before, /device:TPU:6 now
where the time goes in v3:
time: 174 us; the launch traced here: 171 us
  Pallas kernels  171 us (98%)
    pallas_call x1, Pallas kernels, local(): pl.pallas_call(functools.partial(block_kernel, sizes, groups), out_shape=...  114 us
    pallas_call x1, Pallas kernels, local(): pl.pallas_call(hand_over, out_shape=results, in_specs=[anywhere] * 5, out...  57.1 us

profile of v3, /device:TPU:6, one launch (start us, length us, event | category | flops | bytes accessed | tf_op | source)
XLA Modules:
  0.0 171.3 jit_solution(11787463596625685775)
XLA Ops:
  0.6 113.6 %shard_map.137 = (bf16[512,256]{1,0:T(8,128)(2,1)}, bf16[1024,256]{1,0:T(8,128)(2,1)}, bf16[1024,256]{1,0:T(8,128)(2,1)}, bf16[1024,256]{1,0:T(8,128)(2,1)}, f32[3,4,256]{2,1,0:T(4,128)}) custom-call(s32[1,512]{1,0:T(1,128)} %bitcast.5, bf16[512,256]{1,0:T(8,128)(2,1)} %hidden_in.1, bf16[4,256]{1,0:T(4,128)(2,1)} %embedding_in.1, bf16[1024,256]{1,0:T(8,128)(2,1)} %w_in_in.1, ...), custom_call_target="tpu_custom_call" | custom-call | tf_op jit(solution)/shard_map/pallas_call | solution.py:607
  114.2 57.1 %shard_map.138 = (bf16[512,256]{1,0:T(8,128)(2,1)}, bf16[1024,256]{1,0:T(8,128)(2,1)}, bf16[1024,256]{1,0:T(8,128)(2,1)}, bf16[1024,256]{1,0:T(8,128)(2,1)}, f32[3,4,256]{2,1,0:T(4,128)}) custom-call(bf16[512,256]{1,0:T(8,128)(2,1)} %get-tuple-element.10.refs_0_, bf16[1024,256]{1,0:T(8,128)(2,1)} %get-tuple-element.11.refs_1_, ...), custom_call_target="tpu_custom_call" | custom-call | tf_op jit(solution)/shard_map/pallas_call | solution.py:671

commit v4 on v3

--- a/solution.py
+++ b/solution.py
@@ -16,8 +16,8 @@
 FWD_LEFT, FWD_RIGHT = 160, 80
 BWD_LEFT, BWD_RIGHT = 80, 160
 CHUNK = 64
-SENDS = 224
-RECEIVES = 256
+SENDS = 128
+RECEIVES = 160
 
 
 def ring_sizes(count):
@@ -39,9 +39,9 @@
     tokens_ref, hidden_ref, w_in_ref, w_gate_ref, conv_w_ref, order_ref, gain_ref, w_out_ref,
     output_ref, grad_in_ref, grad_gate_ref, grad_out_ref, grad_conv_ref,
     block_in, embed, level0, level1, level2, level3, gate_pre, halo_send, halo_recv, halo_late,
-    gated, both, permute, cot_mix, term_send, term_recv, term_cross, norm_mix, grad_split,
+    gated, both, permute, cot_near, cot_far, cot_mix, term_send, term_recv, term_cross, norm_mix, grad_split,
     grad_gated, up3, up2, up1, product_send, product_recv, up3_low, up0_low, gate_low,
-    send1, recv1, send2, recv2, whole, conv_x, send_sem, recv_sem, local_sem,
+    send1, recv1, send1_late, recv1_late, send2, recv2, whole, conv_x, send_sem, recv_sem, local_sem,
 ):
     xs, zs, ys = sizes
     count = xs * zs * ys
@@ -69,16 +69,16 @@
     def at(x, z, y):
         return {"seq": (x * zs + z) * ys + y}
 
-    first = (ys, zs)
-    second = (zs, ys)
-    me1 = (my_y, my_z)
-    me2 = (my_z, my_y)
-
-    def first_peer(h, t):
-        return at(my_x, my_z, t) if h == 0 else at(my_x, t, my_y)
-
-    def second_peer(h, x, t):
-        return at(x, t, my_y) if h == 0 else at(x, my_z, t)
+    assert ys == zs
+    ring = ys
+    me1 = my_y + core * (my_z - my_y)
+    me2 = my_z + core * (my_y - my_z)
+
+    def first_peer(t):
+        return at(my_x, my_z + core * (t - my_z), t + core * (my_y - t))
+
+    def second_peer(x, t):
+        return at(x, t + core * (my_z - t), my_y + core * (t - my_y))
 
     def top(q):
         return pl.ds(pl.multiple_of(q * eighth, eighth), eighth)
@@ -100,15 +100,12 @@
         greet({"seq": mirror, "ch": q})
     greet({"seq": after})
     greet({"seq": before})
-    for h in range(2):
-        for d in range(1, first[h]):
-            greet(first_peer(h, lax.rem(me1[h] + d, first[h])))
-    for dx in range(1, xs):
-        x = lax.rem(my_x + dx, xs)
-        for dz in range(zs):
-            greet(at(x, lax.rem(my_z + dz, zs), my_y))
-        for dy in range(1, ys):
-            greet(at(x, my_z, lax.rem(my_y + dy, ys)))
+    for d in range(1, ring):
+        greet(first_peer(lax.rem(me1 + d, ring)))
+    for dx in range(xs):
+        for d in range(ring):
+            if dx or d:
+                greet(second_peer(lax.rem(my_x + dx, xs), lax.rem(me2 + d, ring)))
 
     pending = []
     bases = {}
@@ -138,7 +135,7 @@
         ("tokens", tokens_in, tokens_ref),
         ("embedding", embedding_in, embed.at[pl.ds(0, 4)]),
         ("hidden", hidden_in, hidden_ref),
-        ("cot", cot_in.at[pl.ds(0, half)], cot_mix.at[pl.ds(0, half)]),
+        ("cot", cot_in.at[pl.ds(0, half)], cot_near),
         ("order", order_in, order_ref),
         ("w_in", w_in_in, w_in_ref),
         ("w_gate", w_gate_in, w_gate_ref),
@@ -177,9 +174,9 @@
 
     for i in range(3):
         gather_send(i, ch, across)
-        gather_send(i, ch, sibling)
+    send(block_in.at[ch], block_in.at[ch], gather + ch, {"ch": sibling})
     cot_sem = base("cot", 1)
-    send(cot_in.at[pl.ds(half, half)], cot_mix.at[pl.ds(half, half)], cot_sem, {"seq": mirror})
+    send(cot_in.at[pl.ds(half, half)], cot_far, cot_sem, {"seq": mirror})
 
     loads["order"].wait()
     for start in range(0, full, 128):
@@ -191,6 +188,18 @@
         == 2 * eighth - 1
     ).astype(F32).astype(BF16)
 
+    def terms(source, part):
+        value = dot(source[...], w_out_ref[...], (1, 1)).astype(BF16)
+        for q in range(groups):
+            start = q * eighth if part == 0 else half - eighth - q * eighth
+            span = slice(part * eighth, (part + 1) * eighth)
+            term_send[q, span, :] = value[start : start + eighth]
+            cot_mix[q, span, :] = source[start : start + eighth, :]
+
+    loads["cot"].wait()
+    loads["w_out"].wait()
+    terms(cot_near, 0)
+
     def project(i, weights):
         start, size = parts[i]
         total = jnp.zeros((size, width), F32)
@@ -205,7 +214,8 @@
         gather_send(i, across, sibling)
     for i in range(2):
         start, size = parts[i]
-        gather_wait(i, sibling)
+        if i == 0:
+            arrived(block_in.at[sibling], gather + sibling)
         gather_wait(i, diagonal)
         projected = project(i, w_in_ref).astype(BF16)
         level0[FWD_LEFT + start : FWD_LEFT + start + size, :] = projected.astype(F32)
@@ -219,17 +229,9 @@
         start, size = parts[i]
         gate_pre[start : start + size, :] = project(i, w_gate_ref)
 
-    loads["w_out"].wait()
-    loads["cot"].wait()
-    arrived(cot_mix.at[pl.ds(half, half)], cot_sem)
-    for q in range(groups):
-        low = rows - eighth - q * eighth
-        for part, start in enumerate((q * eighth, low)):
-            term_send[q, part * eighth : (part + 1) * eighth, :] = dot(
-                cot_mix[start : start + eighth, :], w_out_ref[...], (1, 1)
-            ).astype(BF16)
+    arrived(cot_far, cot_sem)
+    terms(cot_far, 1)
     term = base("term", 3)
-    gather_wait(2, sibling)
     gather_wait(2, diagonal)
     for i in range(2):
         target = i * 2 + 1 - core
@@ -307,8 +309,7 @@
     inv_scale = lax.rsqrt(jnp.mean(combined * combined, axis=1, keepdims=True) + EPSILON)
     hat = combined * inv_scale
     normalized = (hat * gain_ref[...]).astype(BF16)
-    norm_mix[top(ch), :] = normalized[:eighth]
-    norm_mix[bottom(ch), :] = normalized[eighth:]
+    norm_mix[ch] = normalized
     row_total = jnp.sum(scaled * hat, axis=1, keepdims=True)
     grad_comb = (inv_scale * (scaled - hat * (row_total * (1.0 / full)))).astype(BF16)
     turned = dot(flip, dot(grad_comb, permute[...], (1, 1)).astype(BF16), (1, 0))
@@ -326,15 +327,13 @@
         send(grad_split.at[q, pl.ds(0, eighth)], grad_gated.at[top(ch)], back + ch, {"ch": q})
     grad_gated[top(ch), :] = grad_split[ch, 0:eighth, :]
 
-    norm = base("norm", 2 * groups)
+    norm = base("norm", groups)
 
     def norm_send(q, target):
-        send(norm_mix.at[top(q)], norm_mix.at[top(q)], norm + q, {"ch": target})
-        send(norm_mix.at[bottom(q)], norm_mix.at[bottom(q)], norm + groups + q, {"ch": target})
+        send(norm_mix.at[q], norm_mix.at[q], norm + q, {"ch": target})
 
     def norm_wait(q):
-        arrived(norm_mix.at[top(q)], norm + q)
-        arrived(norm_mix.at[bottom(q)], norm + groups + q)
+        arrived(norm_mix.at[q], norm + q)
 
     norm_send(ch, across)
     norm_send(ch, sibling)
@@ -342,133 +341,109 @@
     norm_send(across, sibling)
 
     conv_rows = 16
-    size = full // ys
-    part = size // zs
-    names = ("out", "gate", "in")
-    early, late = ("out", "gate"), ("in",)
-
-    def span1(name):
-        return pl.ds(0, size + (conv_rows if name == "in" else 0))
-
-    def sem1(name, h, k):
-        return base("sum " + name, 2 * ys) + h * ys + k
-
-    def spread(name, value):
-        g = names.index(name)
-        for h in range(2):
-            for k in range(first[h]):
-                send1[g, h, k, 0:size, :] = value[k * size : (k + 1) * size, 128 * h : 128 * h + 128].astype(BF16)
-        for d in range(1, ys):
-            for h in range(2):
-                t = lax.rem(me1[h] + d, first[h])
-                send(
-                    send1.at[g, h, t, span1(name)], recv1.at[g, h, me1[h], span1(name)],
-                    sem1(name, h, me1[h]), first_peer(h, t),
-                )
-
-    def tall2(unit, same):
-        return len(unit) * part + (conv_rows if same and unit is late else 0)
+    size = full // ring
+    part = size // ring
+    early, late = (0, 2), (2, 1)
+    first_send = {early: send1, late: send1_late}
+    first_recv = {early: recv1, late: recv1_late}
+
+    def spread(unit, values):
+        for k in range(ring):
+            for g, value in enumerate(values):
+                first_send[unit][k, g * size : (g + 1) * size, :] = value[k * size : (k + 1) * size].astype(BF16)
+        for d in range(1, ring):
+            t = lax.rem(me1 + d, ring)
+            send(first_send[unit].at[t], first_recv[unit].at[me1], sem1(unit, me1), first_peer(t))
+
+    def sem1(unit, k):
+        return base(("sum", unit), ring) + k
 
     def rows2(unit, same):
-        return pl.ds(names.index(unit[0]) * part, tall2(unit, same))
-
-    def sem2(unit, h, k):
-        return base("over " + unit[0], 2 * xs * zs) + h * xs * zs + k
+        return pl.ds(unit[0] * part, unit[1] * part + (conv_rows if same and unit is late else 0))
+
+    def sem2(unit, k):
+        return base(("over", unit), xs * ring) + k
 
     def second_sum(unit):
-        for h in range(2):
-            for name in unit:
-                g = names.index(name)
-                total = send1[g, h, me1[h], 0:size, :].astype(F32)
-                for d in range(1, first[h]):
-                    k = lax.rem(me1[h] + d, first[h])
-                    arrived(recv1.at[g, h, k, span1(name)], sem1(name, h, k))
-                    total = total + recv1[g, h, k, 0:size, :].astype(F32)
-                total = total.astype(BF16)
-                for k in range(second[h]):
-                    send2[h, k, g * part : (g + 1) * part, :] = total[k * part : (k + 1) * part]
-            if unit is late:
-                recv1[2, h, me1[h], size:, :] = send1[2, h, me1[h], size:, :]
-                tail = jnp.zeros((conv_rows, 128), F32)
-                for k in range(first[h]):
-                    tail = tail + recv1[2, h, k, size:, :].astype(F32)
-                for k in range(second[h]):
-                    send2[h, k, 3 * part :, :] = tail.astype(BF16)
-            slot = my_x * second[h] + me2[h]
-            for dx in reversed(range(xs)):
-                for dt in range(second[h]):
-                    if dx or dt:
-                        x = lax.rem(my_x + dx, xs)
-                        t = lax.rem(me2[h] + dt, second[h])
-                        span = rows2(unit, dx == 0)
-                        send(send2.at[h, t, span], recv2.at[h, slot, span], sem2(unit, h, slot), second_peer(h, x, t))
-            span = rows2(unit, True)
-            recv2[h, slot, span, :] = send2[h, me2[h], span, :]
-
-    def sem3(unit, h, k):
-        return base("gather2 " + unit[0], 2 * zs) + h * zs + k
-
-    conv_sem = base("conv", 2 * xs)
-
-    def span3(unit):
-        return pl.ds(names.index(unit[0]) * part, len(unit) * part)
+        tall = unit[1] * size
+        total = first_send[unit][me1, 0:tall, :].astype(F32)
+        for d in range(1, ring):
+            k = lax.rem(me1 + d, ring)
+            arrived(first_recv[unit].at[k], sem1(unit, k))
+            total = total + first_recv[unit][k, 0:tall, :].astype(F32)
+        total = total.astype(BF16)
+        for k in range(ring):
+            for g in range(unit[1]):
+                low = (unit[0] + g) * part
+                send2[k, low : low + part, :] = total[g * size + k * part : g * size + (k + 1) * part]
+        if unit is late:
+            recv1_late[me1, size:, :] = send1_late[me1, size:, :]
+            tail = jnp.zeros((conv_rows, width), F32)
+            for k in range(ring):
+                tail = tail + recv1_late[k, size:, :].astype(F32)
+            for k in range(ring):
+                send2[k, 3 * part :, :] = tail.astype(BF16)
+        slot = my_x * ring + me2
+        for dx in reversed(range(xs)):
+            for d in range(ring):
+                if dx or d:
+                    x = lax.rem(my_x + dx, xs)
+                    t = lax.rem(me2 + d, ring)
+                    span = rows2(unit, dx == 0)
+                    send(send2.at[t, span], recv2.at[slot, span], sem2(unit, slot), second_peer(x, t))
+        span = rows2(unit, True)
+        recv2[slot, span, :] = send2[me2, span, :]
+
+    def sem3(unit, k):
+        return base(("gather2", unit), ring) + k
+
+    def sem4(unit, k):
+        return base(("gather1", unit), ring) + k
+
+    conv_sem = base("conv", xs)
+
+    def finished(unit, k, m=None):
+        if unit is late:
+            if m is None:
+                return grad_in_ref.at[pl.ds(pl.multiple_of(k * size, size), size)]
+            return grad_in_ref.at[pl.ds(pl.multiple_of(k * size + m * part, part), part)]
+        return whole.at[k] if m is None else whole.at[k, m]
 
     def second_gather(unit):
-        for h in range(2):
-            for dx in range(xs):
-                for dt in range(second[h]):
-                    if dx or dt:
-                        k = lax.rem(my_x + dx, xs) * second[h] + lax.rem(me2[h] + dt, second[h])
-                        arrived(recv2.at[h, k, rows2(unit, dx == 0)], sem2(unit, h, k))
-            total = jnp.zeros((len(unit) * part, 128), F32)
-            for k in range(xs * second[h]):
-                total = total + recv2[h, k, span3(unit), :].astype(F32)
-            whole[names.index(unit[0]) // 2, h, me1[h], me2[h], 0 : len(unit) * part] = total.astype(BF16)
-            for d in range(1, second[h]):
-                t = lax.rem(me2[h] + d, second[h])
-                here = whole.at[names.index(unit[0]) // 2, h, me1[h], me2[h], pl.ds(0, len(unit) * part)]
-                send(here, here, sem3(unit, h, me2[h]), second_peer(h, my_x, t))
-            if unit is late:
-                tail = jnp.zeros((conv_rows, 128), F32)
-                for t in range(second[h]):
-                    tail = tail + recv2[h, my_x * second[h] + t, 3 * part :, :].astype(F32)
-                conv_x[h, my_x] = tail.astype(BF16)
-                for dx in range(1, xs):
-                    here = conv_x.at[h, my_x]
-                    send(here, here, conv_sem + h * xs + my_x, at(lax.rem(my_x + dx, xs), my_z, my_y))
-
-    def sem4(unit, h, k):
-        return base("gather1 " + unit[0], 2 * ys) + h * ys + k
-
-    def block4(unit, h, k):
-        return whole.at[names.index(unit[0]) // 2, h, k, pl.ds(0, zs), pl.ds(0, len(unit) * part)]
+        for dx in range(xs):
+            for d in range(ring):
+                if dx or d:
+                    k = lax.rem(my_x + dx, xs) * ring + lax.rem(me2 + d, ring)
+                    arrived(recv2.at[k, rows2(unit, dx == 0)], sem2(unit, k))
+        span = rows2(unit, False)
+        total = jnp.zeros((unit[1] * part, width), F32)
+        for k in range(xs * ring):
+            total = total + recv2[k, span, :].astype(F32)
+        here = finished(unit, me1, me2)
+        here[...] = total.astype(BF16)
+        for d in range(1, ring):
+            send(here, here, sem3(unit, me2), second_peer(my_x, lax.rem(me2 + d, ring)))
+        if unit is late:
+            tail = jnp.zeros((conv_rows, width), F32)
+            for t in range(ring):
+                tail = tail + recv2[my_x * ring + t, 3 * part :, :].astype(F32)
+            conv_x[my_x] = tail.astype(BF16)
+            for dx in range(1, xs):
+                here = conv_x.at[my_x]
+                send(here, here, conv_sem + my_x, at(lax.rem(my_x + dx, xs), my_z, my_y))
 
     def first_gather(unit):
-        u = names.index(unit[0]) // 2
-        for h in range(2):
-            for d in range(1, second[h]):
-                k = lax.rem(me2[h] + d, second[h])
-                arrived(whole.at[u, h, me1[h], k, pl.ds(0, len(unit) * part)], sem3(unit, h, k))
-            for d in range(1, first[h]):
-                t = lax.rem(me1[h] + d, first[h])
-                send(block4(unit, h, me1[h]), block4(unit, h, me1[h]), sem4(unit, h, me1[h]), first_peer(h, t))
-
-    outs = (grad_out_ref, grad_gate_ref, grad_in_ref)
-
-    def place_rows(unit, h, k):
-        for i, name in enumerate(unit):
-            block = whole[names.index(unit[0]) // 2, h, k, :, i * part : (i + 1) * part, :]
-            at_row = pl.multiple_of(k * size, size)
-            outs[names.index(name)][pl.ds(at_row, size), 128 * h : 128 * h + 128] = block.reshape(size, 128)
+        for d in range(1, ring):
+            k = lax.rem(me2 + d, ring)
+            arrived(finished(unit, me1, k), sem3(unit, k))
+        here = finished(unit, me1)
+        for d in range(1, ring):
+            send(here, here, sem4(unit, me1), first_peer(lax.rem(me1 + d, ring)))
 
     def finish(unit):
-        for h in range(2):
-            place_rows(unit, h, me1[h])
-        for d in range(1, ys):
-            for h in range(2):
-                k = lax.rem(me1[h] + d, first[h])
-                arrived(block4(unit, h, k), sem4(unit, h, k))
-                place_rows(unit, h, k)
+        for d in range(1, ring):
+            k = lax.rem(me1 + d, ring)
+            arrived(finished(unit, k), sem4(unit, k))
 
     for d in range(1, groups):
         q = lax.rem(ch + d, groups)
@@ -497,8 +472,8 @@
 
     norm_wait(sibling)
     norm_wait(diagonal)
-    spread("out", dot(norm_mix[...], cot_mix[...], (0, 0)))
-    spread("gate", against_input(gate_low[...]))
+    normalized_rows = norm_mix[...].reshape(rows, full)
+    spread(early, (dot(normalized_rows, cot_mix[...].reshape(rows, width), (0, 0)), against_input(gate_low[...])))
 
     arrived(halo_late.at[pl.ds(BWD_LEFT, BWD_RIGHT)], halo_back)
     arrived(halo_late.at[pl.ds(0, BWD_LEFT)], halo_back + 1)
@@ -529,18 +504,21 @@
                 total = total + jnp.sum(term_product.reshape(tall // 8, 8, width), axis=0)
             taps.append(jnp.sum(total, axis=0, keepdims=True))
     taps = jnp.concatenate(taps + [jnp.zeros((conv_rows - 12, width), F32)], axis=0).astype(BF16)
-    for h in range(2):
-        for k in range(first[h]):
-            send1[2, h, k, size : size + conv_rows, :] = taps[:, 128 * h : 128 * h + 128]
-    spread("in", against_input(up0_low[...]))
+    for k in range(ring):
+        send1_late[k, size : size + conv_rows, :] = taps
+    spread(late, (against_input(up0_low[...]),))
 
     second_sum(early)
 
-    product = dot(norm_mix[...], w_out_ref[...], (1, 0))
-    product_send[...] = product[half:].astype(BF16)
+    product = dot(norm_mix[...].reshape(rows, full), w_out_ref[...], (1, 0))
+    for q in range(groups):
+        near = product[q * 2 * eighth : q * 2 * eighth + eighth]
+        low = q * eighth
+        output_ref[low : low + eighth, :] = (block_in[ch, low : low + eighth, :].astype(F32) + near).astype(BF16)
+        low = half - eighth - q * eighth
+        product_send[low : low + eighth, :] = product[q * 2 * eighth + eighth : (q + 1) * 2 * eighth].astype(BF16)
     product_sem = base("product", 1)
     send(product_send, product_recv, product_sem, {"seq": mirror})
-    output_ref[0:half, :] = (block_in[ch, 0:half, :].astype(F32) + product[:half]).astype(BF16)
     store_out(output_ref.at[pl.ds(0, half)], output_out.at[pl.ds(0, half)])
 
     second_sum(late)
@@ -553,17 +531,19 @@
     second_gather(late)
     first_gather(early)
     first_gather(late)
-    for h in range(2):
-        for dx in range(1, xs):
-            x = lax.rem(my_x + dx, xs)
-            arrived(conv_x.at[h, x], conv_sem + h * xs + x)
-        tail = jnp.zeros((conv_rows, 128), F32)
-        for x in range(xs):
-            tail = tail + conv_x[h, x].astype(F32)
-        for level in range(3):
-            grad_conv_ref[level, :, 128 * h : 128 * h + 128] = tail[4 * level : 4 * level + 4]
+    for dx in range(1, xs):
+        x = lax.rem(my_x + dx, xs)
+        arrived(conv_x.at[x], conv_sem + x)
+    tail = jnp.zeros((conv_rows, width), F32)
+    for x in range(xs):
+        tail = tail + conv_x[x].astype(F32)
+    for level in range(3):
+        grad_conv_ref[level] = tail[4 * level : 4 * level + 4]
     store_out(grad_conv_ref, grad_conv_out)
     finish(early)
+    for k in range(ring):
+        for g, target in enumerate((grad_out_ref, grad_gate_ref)):
+            target[k * size : (k + 1) * size, :] = whole[k, :, g * part : (g + 1) * part, :].reshape(size, width)
     store_out(grad_out_ref, grad_out_out)
     store_out(grad_gate_ref, grad_gate_out)
     finish(late)
@@ -575,12 +555,16 @@
 
 
 def hand_over(*refs):
-    count = len(refs) // 2
-    sems = refs[-1]
-    copies = [pltpu.make_async_copy(refs[i], refs[count + i], sems.at[i]) for i in range(count)]
-    for copy in copies:
+    count = len(refs) // 3
+    given, results, stages, sems = refs[:count], refs[count : 2 * count], refs[2 * count : 3 * count], refs[-1]
+    loads = [pltpu.make_async_copy(given[i], stages[i], sems.at[0, i]) for i in range(count)]
+    stores = [pltpu.make_async_copy(stages[i], results[i], sems.at[1, i]) for i in range(count)]
+    for copy in loads:
         copy.start()
-    for copy in copies:
+    for load, store in zip(loads, stores):
+        load.wait()
+        store.start()
+    for copy in stores:
         copy.wait()
 
 
@@ -636,11 +620,13 @@
             held(rows, width),
             held(groups, 2 * eighth, width),
             held(full, full),
-            held(rows, width),
+            held(rows // 2, width),
+            held(rows // 2, width),
+            held(groups, 2 * eighth, width),
             held(groups, 2 * eighth, full),
             held(2, 2 * eighth, full),
             held(2 * eighth, full),
-            held(rows, full),
+            held(groups, 2 * eighth, full),
             held(groups, 2 * eighth, width),
             held(rows, width),
             held(extended, width, dtype=F32),
@@ -651,12 +637,14 @@
             held(rows, width),
             held(rows, width),
             held(rows, width),
-            held(3, 2, ys, size + 16, 128),
-            held(3, 2, ys, size + 16, 128),
-            held(2, zs, 3 * part + 16, 128),
-            held(2, xs * zs, 3 * part + 16, 128),
-            held(2, 2, ys, zs, 2 * part, 128),
-            held(2, xs, 16, 128),
+            held(ys, 2 * size, width),
+            held(ys, 2 * size, width),
+            held(ys, size + 16, width),
+            held(ys, size + 16, width),
+            held(zs, 3 * part + 16, width),
+            held(xs * zs, 3 * part + 16, width),
+            held(ys, zs, 2 * part, width),
+            held(xs, 16, width),
             dma((SENDS,)),
             dma((RECEIVES,)),
             dma((16,)),
@@ -673,7 +661,7 @@
         out_shape=results,
         in_specs=[anywhere] * 5,
         out_specs=(anywhere,) * 5,
-        scratch_shapes=[dma((5,))],
+        scratch_shapes=[held(*result.shape, dtype=result.dtype) for result in results] + [dma((2, 5))],
         compiler_params=pltpu.CompilerParams(vmem_limit_bytes=60 * 1024 * 1024),
     )(*computed)
 

time: 174 us -> 122 us (0.70)
  the two profiles are of different devices: /device:TPU:6 before, /device:TPU:18 now
where the time goes in v4:
time: 122 us; the launch traced here: 121 us
  Pallas kernels  121 us (99%)
    pallas_call x1, Pallas kernels, local(): pl.pallas_call(functools.partial(block_kernel, sizes, groups), out_shape=...  118 us

profile of v4, /device:TPU:18, one launch (start us, length us, event | category | flops | bytes accessed | tf_op | source)
XLA Modules:
  0.0 121.4 jit_solution(10805819446059667395)
XLA Ops:
  0.6 118.4 %shard_map.137 = (bf16[512,256]{1,0:T(8,128)(2,1)}, bf16[1024,256]{1,0:T(8,128)(2,1)}, bf16[1024,256]{1,0:T(8,128)(2,1)}, bf16[1024,256]{1,0:T(8,128)(2,1)}, f32[3,4,256]{2,1,0:T(4,128)}) custom-call(s32[1,512]{1,0:T(1,128)} %bitcast.5, bf16[512,256]{1,0:T(8,128)(2,1)} %hidden_in.1, bf16[4,256]{1,0:T(4,128)(2,1)} %embedding_in.1, bf16[1024,256]{1,0:T(8,128)(2,1)} %w_in_in.1, ...), custom_call_target="tpu_custom_call" | custom-call | tf_op jit(solution)/shard_map/pallas_call | solution.py:591
  119.0 2.4 %shard_map.138 = (bf16[512,256]{1,0:T(8,128)(2,1)}, bf16[1024,256]{1,0:T(8,128)(2,1)}, bf16[1024,256]{1,0:T(8,128)(2,1)}, bf16[1024,256]{1,0:T(8,128)(2,1)}, f32[3,4,256]{2,1,0:T(4,128)}) custom-call(bf16[512,256]{1,0:T(8,128)(2,1)} %get-tuple-element.10.refs_0_, bf16[1024,256]{1,0:T(8,128)(2,1)} %get-tuple-element.11.refs_1_, ...), custom_call_target="tpu_custom_call" | custom-call | tf_op jit(solution)/shard_map/pallas_call | solution.py:659

commit v5 on v4

--- a/solution.py
+++ b/solution.py
@@ -16,8 +16,8 @@
 FWD_LEFT, FWD_RIGHT = 160, 80
 BWD_LEFT, BWD_RIGHT = 80, 160
 CHUNK = 64
-SENDS = 128
-RECEIVES = 160
+SENDS = 272
+RECEIVES = 304
 
 
 def ring_sizes(count):
@@ -41,7 +41,7 @@
     block_in, embed, level0, level1, level2, level3, gate_pre, halo_send, halo_recv, halo_late,
     gated, both, permute, cot_near, cot_far, cot_mix, term_send, term_recv, term_cross, norm_mix, grad_split,
     grad_gated, up3, up2, up1, product_send, product_recv, up3_low, up0_low, gate_low,
-    send1, recv1, send1_late, recv1_late, send2, recv2, whole, conv_x, send_sem, recv_sem, local_sem,
+    send1, recv1, send2, recv2, conv_x, send_sem, recv_sem, local_sem,
 ):
     xs, zs, ys = sizes
     count = xs * zs * ys
@@ -71,14 +71,14 @@
 
     assert ys == zs
     ring = ys
-    me1 = my_y + core * (my_z - my_y)
-    me2 = my_z + core * (my_y - my_z)
-
-    def first_peer(t):
-        return at(my_x, my_z + core * (t - my_z), t + core * (my_y - t))
-
-    def second_peer(x, t):
-        return at(x, t + core * (my_z - t), my_y + core * (t - my_y))
+    me1 = (my_y, my_z)
+    me2 = (my_z, my_y)
+
+    def first_peer(h, t):
+        return at(my_x, my_z, t) if h == 0 else at(my_x, t, my_y)
+
+    def second_peer(h, x, t):
+        return at(x, t, my_y) if h == 0 else at(x, my_z, t)
 
     def top(q):
         return pl.ds(pl.multiple_of(q * eighth, eighth), eighth)
@@ -100,12 +100,15 @@
         greet({"seq": mirror, "ch": q})
     greet({"seq": after})
     greet({"seq": before})
-    for d in range(1, ring):
-        greet(first_peer(lax.rem(me1 + d, ring)))
-    for dx in range(xs):
+    for h in range(2):
+        for d in range(1, ring):
+            greet(first_peer(h, lax.rem(me1[h] + d, ring)))
+    for dx in range(1, xs):
+        x = lax.rem(my_x + dx, xs)
         for d in range(ring):
-            if dx or d:
-                greet(second_peer(lax.rem(my_x + dx, xs), lax.rem(me2 + d, ring)))
+            greet(second_peer(0, x, lax.rem(my_z + d, ring)))
+        for d in range(1, ring):
+            greet(second_peer(1, x, lax.rem(my_y + d, ring)))
 
     pending = []
     bases = {}
@@ -337,113 +340,124 @@
 
     norm_send(ch, across)
     norm_send(ch, sibling)
-    norm_wait(across)
-    norm_send(across, sibling)
 
     conv_rows = 16
     size = full // ring
     part = size // ring
-    early, late = (0, 2), (2, 1)
-    first_send = {early: send1, late: send1_late}
-    first_recv = {early: recv1, late: recv1_late}
-
-    def spread(unit, values):
-        for k in range(ring):
-            for g, value in enumerate(values):
-                first_send[unit][k, g * size : (g + 1) * size, :] = value[k * size : (k + 1) * size].astype(BF16)
+    lanes = width // 2
+    of_out, of_gate, late = 0, 1, 2
+    finished = (grad_out_ref, grad_gate_ref, grad_in_ref)
+    results = (grad_out_out, grad_gate_out, grad_in_out)
+
+    def side(h):
+        return slice(lanes * h, lanes * h + lanes)
+
+    def span1(u):
+        return pl.ds(0, size + (conv_rows if u == late else 0))
+
+    def sem1(u, h, k):
+        return base(("sum", u), 2 * ring) + h * ring + k
+
+    def spread(u, value):
+        for h in range(2):
+            for k in range(ring):
+                send1[u, h, k, 0:size, :] = value[k * size : (k + 1) * size, side(h)].astype(BF16)
         for d in range(1, ring):
-            t = lax.rem(me1 + d, ring)
-            send(first_send[unit].at[t], first_recv[unit].at[me1], sem1(unit, me1), first_peer(t))
-
-    def sem1(unit, k):
-        return base(("sum", unit), ring) + k
-
-    def rows2(unit, same):
-        return pl.ds(unit[0] * part, unit[1] * part + (conv_rows if same and unit is late else 0))
-
-    def sem2(unit, k):
-        return base(("over", unit), xs * ring) + k
-
-    def second_sum(unit):
-        tall = unit[1] * size
-        total = first_send[unit][me1, 0:tall, :].astype(F32)
-        for d in range(1, ring):
-            k = lax.rem(me1 + d, ring)
-            arrived(first_recv[unit].at[k], sem1(unit, k))
-            total = total + first_recv[unit][k, 0:tall, :].astype(F32)
-        total = total.astype(BF16)
-        for k in range(ring):
-            for g in range(unit[1]):
-                low = (unit[0] + g) * part
-                send2[k, low : low + part, :] = total[g * size + k * part : g * size + (k + 1) * part]
-        if unit is late:
-            recv1_late[me1, size:, :] = send1_late[me1, size:, :]
-            tail = jnp.zeros((conv_rows, width), F32)
+            for h in range(2):
+                t = lax.rem(me1[h] + d, ring)
+                send(
+                    send1.at[u, h, t, span1(u)], recv1.at[u, h, me1[h], span1(u)], sem1(u, h, me1[h]),
+                    first_peer(h, t),
+                )
+
+    def span2(u, same):
+        return pl.ds(u * part, part + (conv_rows if same and u == late else 0))
+
+    def sem2(u, h, k):
+        return base(("over", u), 2 * xs * ring) + h * xs * ring + k
+
+    def second_sum(u):
+        for h in range(2):
+            total = send1[u, h, me1[h], 0:size, :].astype(F32)
+            for d in range(1, ring):
+                k = lax.rem(me1[h] + d, ring)
+                arrived(recv1.at[u, h, k, span1(u)], sem1(u, h, k))
+                total = total + recv1[u, h, k, 0:size, :].astype(F32)
+            total = total.astype(BF16)
             for k in range(ring):
-                tail = tail + recv1_late[k, size:, :].astype(F32)
-            for k in range(ring):
-                send2[k, 3 * part :, :] = tail.astype(BF16)
-        slot = my_x * ring + me2
-        for dx in reversed(range(xs)):
-            for d in range(ring):
-                if dx or d:
-                    x = lax.rem(my_x + dx, xs)
-                    t = lax.rem(me2 + d, ring)
-                    span = rows2(unit, dx == 0)
-                    send(send2.at[t, span], recv2.at[slot, span], sem2(unit, slot), second_peer(x, t))
-        span = rows2(unit, True)
-        recv2[slot, span, :] = send2[me2, span, :]
-
-    def sem3(unit, k):
-        return base(("gather2", unit), ring) + k
-
-    def sem4(unit, k):
-        return base(("gather1", unit), ring) + k
-
-    conv_sem = base("conv", xs)
-
-    def finished(unit, k, m=None):
-        if unit is late:
-            if m is None:
-                return grad_in_ref.at[pl.ds(pl.multiple_of(k * size, size), size)]
-            return grad_in_ref.at[pl.ds(pl.multiple_of(k * size + m * part, part), part)]
-        return whole.at[k] if m is None else whole.at[k, m]
-
-    def second_gather(unit):
-        for dx in range(xs):
-            for d in range(ring):
-                if dx or d:
-                    k = lax.rem(my_x + dx, xs) * ring + lax.rem(me2 + d, ring)
-                    arrived(recv2.at[k, rows2(unit, dx == 0)], sem2(unit, k))
-        span = rows2(unit, False)
-        total = jnp.zeros((unit[1] * part, width), F32)
-        for k in range(xs * ring):
-            total = total + recv2[k, span, :].astype(F32)
-        here = finished(unit, me1, me2)
-        here[...] = total.astype(BF16)
-        for d in range(1, ring):
-            send(here, here, sem3(unit, me2), second_peer(my_x, lax.rem(me2 + d, ring)))
-        if unit is late:
-            tail = jnp.zeros((conv_rows, width), F32)
-            for t in range(ring):
-                tail = tail + recv2[my_x * ring + t, 3 * part :, :].astype(F32)
-            conv_x[my_x] = tail.astype(BF16)
-            for dx in range(1, xs):
-                here = conv_x.at[my_x]
-                send(here, here, conv_sem + my_x, at(lax.rem(my_x + dx, xs), my_z, my_y))
-
-    def first_gather(unit):
-        for d in range(1, ring):
-            k = lax.rem(me2 + d, ring)
-            arrived(finished(unit, me1, k), sem3(unit, k))
-        here = finished(unit, me1)
-        for d in range(1, ring):
-            send(here, here, sem4(unit, me1), first_peer(lax.rem(me1 + d, ring)))
-
-    def finish(unit):
-        for d in range(1, ring):
-            k = lax.rem(me1 + d, ring)
-            arrived(finished(unit, k), sem4(unit, k))
+                send2[h, k, u * part : (u + 1) * part, :] = total[k * part : (k + 1) * part]
+            if u == late:
+                recv1[u, h, me1[h], size:, :] = send1[u, h, me1[h], size:, :]
+                tail = jnp.zeros((conv_rows, lanes), F32)
+                for k in range(ring):
+                    tail = tail + recv1[u, h, k, size:, :].astype(F32)
+                for k in range(ring):
+                    send2[h, k, 3 * part :, :] = tail.astype(BF16)
+            slot = my_x * ring + me2[h]
+            for dx in reversed(range(xs)):
+                for d in range(ring):
+                    if dx or d:
+                        x = lax.rem(my_x + dx, xs)
+                        t = lax.rem(me2[h] + d, ring)
+                        span = span2(u, dx == 0)
+                        send(send2.at[h, t, span], recv2.at[h, slot, span], sem2(u, h, slot), second_peer(h, x, t))
+            span = span2(u, True)
+            recv2[h, slot, span, :] = send2[h, me2[h], span, :]
+
+    def sem3(u, h, k):
+        return base(("gather2", u), 2 * ring) + h * ring + k
+
+    def sem4(u, h, k):
+        return base(("gather1", u), 2 * ring) + h * ring + k
+
+    conv_sem = base("conv", 2 * xs)
+
+    def rows_of(k, m=None):
+        if m is None:
+            return pl.ds(pl.multiple_of(k * size, size), size)
+        return pl.ds(pl.multiple_of(k * size + m * part, part), part)
+
+    def done(u, h, k, m=None):
+        return finished[u].at[rows_of(k, m), pl.ds(lanes * h, lanes)]
+
+    def second_gather(u):
+        for h in range(2):
+            for dx in range(xs):
+                for d in range(ring):
+                    if dx or d:
+                        k = lax.rem(my_x + dx, xs) * ring + lax.rem(me2[h] + d, ring)
+                        arrived(recv2.at[h, k, span2(u, dx == 0)], sem2(u, h, k))
+            total = jnp.zeros((part, lanes), F32)
+            for k in range(xs * ring):
+                total = total + recv2[h, k, span2(u, False), :].astype(F32)
+            here = done(u, h, me1[h], me2[h])
+            here[...] = total.astype(BF16)
+            for d in range(1, ring):
+                send(here, here, sem3(u, h, me2[h]), second_peer(h, my_x, lax.rem(me2[h] + d, ring)))
+            if u == late:
+                tail = jnp.zeros((conv_rows, lanes), F32)
+                for t in range(ring):
+                    tail = tail + recv2[h, my_x * ring + t, 3 * part :, :].astype(F32)
+                conv_x[h, my_x] = tail.astype(BF16)
+                for dx in range(1, xs):
+                    here = conv_x.at[h, my_x]
+                    send(here, here, conv_sem + h * xs + my_x, at(lax.rem(my_x + dx, xs), my_z, my_y))
+
+    def first_gather(u):
+        for h in range(2):
+            for d in range(1, ring):
+                k = lax.rem(me2[h] + d, ring)
+                arrived(done(u, h, me1[h], k), sem3(u, h, k))
+            here = done(u, h, me1[h])
+            for d in range(1, ring):
+                send(here, here, sem4(u, h, me1[h]), first_peer(h, lax.rem(me1[h] + d, ring)))
+
+    def finish(u):
+        for h in range(2):
+            for d in range(1, ring):
+                k = lax.rem(me1[h] + d, ring)
+                arrived(done(u, h, k), sem4(u, h, k))
+        store_out(finished[u], results[u])
 
     for d in range(1, groups):
         q = lax.rem(ch + d, groups)
@@ -470,10 +484,12 @@
     def against_input(value):
         return jnp.concatenate([dot(block_in[k], value, (0, 0)) for k in range(groups)], axis=0)
 
+    norm_wait(across)
+    norm_send(across, sibling)
+    spread(of_gate, against_input(gate_low[...]))
     norm_wait(sibling)
     norm_wait(diagonal)
-    normalized_rows = norm_mix[...].reshape(rows, full)
-    spread(early, (dot(normalized_rows, cot_mix[...].reshape(rows, width), (0, 0)), against_input(gate_low[...])))
+    spread(of_out, dot(norm_mix[...].reshape(rows, full), cot_mix[...].reshape(rows, width), (0, 0)))
 
     arrived(halo_late.at[pl.ds(BWD_LEFT, BWD_RIGHT)], halo_back)
     arrived(halo_late.at[pl.ds(0, BWD_LEFT)], halo_back + 1)
@@ -504,11 +520,12 @@
                 total = total + jnp.sum(term_product.reshape(tall // 8, 8, width), axis=0)
             taps.append(jnp.sum(total, axis=0, keepdims=True))
     taps = jnp.concatenate(taps + [jnp.zeros((conv_rows - 12, width), F32)], axis=0).astype(BF16)
-    for k in range(ring):
-        send1_late[k, size : size + conv_rows, :] = taps
-    spread(late, (against_input(up0_low[...]),))
-
-    second_sum(early)
+    for h in range(2):
+        for k in range(ring):
+            send1[late, h, k, size : size + conv_rows, :] = taps[:, side(h)]
+    spread(late, against_input(up0_low[...]))
+
+    second_sum(of_gate)
 
     product = dot(norm_mix[...].reshape(rows, full), w_out_ref[...], (1, 0))
     for q in range(groups):
@@ -521,35 +538,34 @@
     send(product_send, product_recv, product_sem, {"seq": mirror})
     store_out(output_ref.at[pl.ds(0, half)], output_out.at[pl.ds(0, half)])
 
+    second_sum(of_out)
+    second_gather(of_gate)
     second_sum(late)
-    second_gather(early)
+    second_gather(of_out)
     arrived(product_recv, product_sem)
     output_ref[half:rows, :] = (
         block_in[ch, half:rows, :].astype(F32) + product_recv[...].astype(F32)
     ).astype(BF16)
     store_out(output_ref.at[pl.ds(half, half)], output_out.at[pl.ds(half, half)])
+    first_gather(of_gate)
     second_gather(late)
-    first_gather(early)
+    first_gather(of_out)
     first_gather(late)
-    for dx in range(1, xs):
-        x = lax.rem(my_x + dx, xs)
-        arrived(conv_x.at[x], conv_sem + x)
-    tail = jnp.zeros((conv_rows, width), F32)
-    for x in range(xs):
-        tail = tail + conv_x[x].astype(F32)
-    for level in range(3):
-        grad_conv_ref[level] = tail[4 * level : 4 * level + 4]
+    for h in range(2):
+        for dx in range(1, xs):
+            x = lax.rem(my_x + dx, xs)
+            arrived(conv_x.at[h, x], conv_sem + h * xs + x)
+        tail = jnp.zeros((conv_rows, lanes), F32)
+        for x in range(xs):
+            tail = tail + conv_x[h, x].astype(F32)
+        for level in range(3):
+            grad_conv_ref[level, :, side(h)] = tail[4 * level : 4 * level + 4]
     store_out(grad_conv_ref, grad_conv_out)
-    finish(early)
-    for k in range(ring):
-        for g, target in enumerate((grad_out_ref, grad_gate_ref)):
-            target[k * size : (k + 1) * size, :] = whole[k, :, g * part : (g + 1) * part, :].reshape(size, width)
-    store_out(grad_out_ref, grad_out_out)
-    store_out(grad_gate_ref, grad_gate_out)
-    finish(late)
-    store_out(grad_in_ref, grad_in_out)
+    finish(of_gate)
+    finish(of_out)
     for copy in pending:
         copy.wait_send()
+    finish(late)
     for copy in stores:
         copy.wait()
 
@@ -637,17 +653,14 @@
             held(rows, width),
             held(rows, width),
             held(rows, width),
-            held(ys, 2 * size, width),
-            held(ys, 2 * size, width),
-            held(ys, size + 16, width),
-            held(ys, size + 16, width),
-            held(zs, 3 * part + 16, width),
-            held(xs * zs, 3 * part + 16, width),
-            held(ys, zs, 2 * part, width),
-            held(xs, 16, width),
+            held(3, 2, ys, size + 16, width // 2),
+            held(3, 2, ys, size + 16, width // 2),
+            held(2, zs, 3 * part + 16, width // 2),
+            held(2, xs * zs, 3 * part + 16, width // 2),
+            held(2, xs, 16, width // 2),
             dma((SENDS,)),
             dma((RECEIVES,)),
-            dma((16,)),
+            dma((32,)),
         ],
         compiler_params=pltpu.CompilerParams(
             collective_id=0, has_side_effects=True, vmem_limit_bytes=56 * 1024 * 1024

time: 122 us -> 117 us (0.959)
  the two profiles are of different devices: /device:TPU:18 before, /device:TPU:6 now
where the time goes in v5:
time: 117 us; the launch traced here: 116 us
  Pallas kernels  115 us (98%)
    pallas_call x1, Pallas kernels, local(): pl.pallas_call(functools.partial(block_kernel, sizes, groups), out_shape=...  113 us
    pallas_call x1, Pallas kernels, local(): pl.pallas_call(hand_over, out_shape=results, in_specs=[anywhere] * 5, out...  2.35 us

profile of v5, /device:TPU:6, one launch (start us, length us, event | category | flops | bytes accessed | tf_op | source)
XLA Modules:
  0.0 116.1 jit_solution(6659759696095552402)
XLA Ops:
  0.6 113.1 %shard_map.137 = (bf16[512,256]{1,0:T(8,128)(2,1)}, bf16[1024,256]{1,0:T(8,128)(2,1)}, bf16[1024,256]{1,0:T(8,128)(2,1)}, bf16[1024,256]{1,0:T(8,128)(2,1)}, f32[3,4,256]{2,1,0:T(4,128)}) custom-call(s32[1,512]{1,0:T(1,128)} %bitcast.5, bf16[512,256]{1,0:T(8,128)(2,1)} %hidden_in.1, bf16[4,256]{1,0:T(4,128)(2,1)} %embedding_in.1, bf16[1024,256]{1,0:T(8,128)(2,1)} %w_in_in.1, ...), custom_call_target="tpu_custom_call" | custom-call | tf_op jit(solution)/shard_map/pallas_call | solution.py:607
  113.8 2.4 %shard_map.138 = (bf16[512,256]{1,0:T(8,128)(2,1)}, bf16[1024,256]{1,0:T(8,128)(2,1)}, bf16[1024,256]{1,0:T(8,128)(2,1)}, bf16[1024,256]{1,0:T(8,128)(2,1)}, f32[3,4,256]{2,1,0:T(4,128)}) custom-call(bf16[512,256]{1,0:T(8,128)(2,1)} %get-tuple-element.10.refs_0_, bf16[1024,256]{1,0:T(8,128)(2,1)} %get-tuple-element.11.refs_1_, ...), custom_call_target="tpu_custom_call" | custom-call | tf_op jit(solution)/shard_map/pallas_call | solution.py:672

commit v6 on v5

--- a/solution.py
+++ b/solution.py
@@ -41,7 +41,7 @@
     block_in, embed, level0, level1, level2, level3, gate_pre, halo_send, halo_recv, halo_late,
     gated, both, permute, cot_near, cot_far, cot_mix, term_send, term_recv, term_cross, norm_mix, grad_split,
     grad_gated, up3, up2, up1, product_send, product_recv, up3_low, up0_low, gate_low,
-    send1, recv1, send2, recv2, conv_x, send_sem, recv_sem, local_sem,
+    send1, recv1, send2, recv2, cross_x, send_sem, recv_sem, local_sem,
 ):
     xs, zs, ys = sizes
     count = xs * zs * ys
@@ -370,11 +370,11 @@
                     first_peer(h, t),
                 )
 
-    def span2(u, same):
-        return pl.ds(u * part, part + (conv_rows if same and u == late else 0))
+    def span2(u):
+        return pl.ds(u * part, part + (conv_rows if u == late else 0))
 
     def sem2(u, h, k):
-        return base(("over", u), 2 * xs * ring) + h * xs * ring + k
+        return base(("over", u), 2 * ring) + h * ring + k
 
     def second_sum(u):
         for h in range(2):
@@ -393,24 +393,34 @@
                     tail = tail + recv1[u, h, k, size:, :].astype(F32)
                 for k in range(ring):
                     send2[h, k, 3 * part :, :] = tail.astype(BF16)
-            slot = my_x * ring + me2[h]
-            for dx in reversed(range(xs)):
-                for d in range(ring):
-                    if dx or d:
-                        x = lax.rem(my_x + dx, xs)
-                        t = lax.rem(me2[h] + d, ring)
-                        span = span2(u, dx == 0)
-                        send(send2.at[h, t, span], recv2.at[h, slot, span], sem2(u, h, slot), second_peer(h, x, t))
-            span = span2(u, True)
-            recv2[h, slot, span, :] = send2[h, me2[h], span, :]
+            span = span2(u)
+            for d in range(1, ring):
+                t = lax.rem(me2[h] + d, ring)
+                send(send2.at[h, t, span], recv2.at[h, me2[h], span], sem2(u, h, me2[h]), second_peer(h, my_x, t))
+            recv2[h, me2[h], span, :] = send2[h, me2[h], span, :]
+
+    def sem_x(u, h, x):
+        return base(("cross", u), 2 * xs) + h * xs + x
+
+    def cross(u):
+        span = span2(u)
+        for h in range(2):
+            for d in range(1, ring):
+                k = lax.rem(me2[h] + d, ring)
+                arrived(recv2.at[h, k, span], sem2(u, h, k))
+            total = recv2[h, 0, span, :].astype(F32)
+            for k in range(1, ring):
+                total = total + recv2[h, k, span, :].astype(F32)
+            here = cross_x.at[h, my_x, span]
+            here[...] = total.astype(BF16)
+            for dx in range(1, xs):
+                send(here, here, sem_x(u, h, my_x), at(lax.rem(my_x + dx, xs), my_z, my_y))
 
     def sem3(u, h, k):
         return base(("gather2", u), 2 * ring) + h * ring + k
 
     def sem4(u, h, k):
         return base(("gather1", u), 2 * ring) + h * ring + k
-
-    conv_sem = base("conv", 2 * xs)
 
     def rows_of(k, m=None):
         if m is None:
@@ -421,27 +431,22 @@
         return finished[u].at[rows_of(k, m), pl.ds(lanes * h, lanes)]
 
     def second_gather(u):
+        span = span2(u)
         for h in range(2):
-            for dx in range(xs):
-                for d in range(ring):
-                    if dx or d:
-                        k = lax.rem(my_x + dx, xs) * ring + lax.rem(me2[h] + d, ring)
-                        arrived(recv2.at[h, k, span2(u, dx == 0)], sem2(u, h, k))
-            total = jnp.zeros((part, lanes), F32)
-            for k in range(xs * ring):
-                total = total + recv2[h, k, span2(u, False), :].astype(F32)
+            for dx in range(1, xs):
+                x = lax.rem(my_x + dx, xs)
+                arrived(cross_x.at[h, x, span], sem_x(u, h, x))
+            total = cross_x[h, 0, span, :].astype(F32)
+            for x in range(1, xs):
+                total = total + cross_x[h, x, span, :].astype(F32)
             here = done(u, h, me1[h], me2[h])
-            here[...] = total.astype(BF16)
+            here[...] = total[0:part].astype(BF16)
             for d in range(1, ring):
                 send(here, here, sem3(u, h, me2[h]), second_peer(h, my_x, lax.rem(me2[h] + d, ring)))
             if u == late:
-                tail = jnp.zeros((conv_rows, lanes), F32)
-                for t in range(ring):
-                    tail = tail + recv2[h, my_x * ring + t, 3 * part :, :].astype(F32)
-                conv_x[h, my_x] = tail.astype(BF16)
-                for dx in range(1, xs):
-                    here = conv_x.at[h, my_x]
-                    send(here, here, conv_sem + h * xs + my_x, at(lax.rem(my_x + dx, xs), my_z, my_y))
+                for level in range(3):
+                    low = part + 4 * level
+                    grad_conv_ref[level, :, side(h)] = total[low : low + 4]
 
     def first_gather(u):
         for h in range(2):
@@ -450,14 +455,29 @@
                 arrived(done(u, h, me1[h], k), sem3(u, h, k))
             here = done(u, h, me1[h])
             for d in range(1, ring):
-                send(here, here, sem4(u, h, me1[h]), first_peer(h, lax.rem(me1[h] + d, ring)))
+                if u == late or d != ring // 2:
+                    send(here, here, sem4(u, h, me1[h]), first_peer(h, lax.rem(me1[h] + d, ring)))
+
+    def relay(u):
+        for h in range(2):
+            k = lax.rem(me1[h] + ring // 2 - 1, ring)
+            here = done(u, h, k)
+            if ring > 2:
+                arrived(here, sem4(u, h, k))
+            send(here, here, sem4(u, h, k), first_peer(h, lax.rem(me1[h] + ring - 1, ring)))
 
     def finish(u):
         for h in range(2):
             for d in range(1, ring):
                 k = lax.rem(me1[h] + d, ring)
-                arrived(done(u, h, k), sem4(u, h, k))
-        store_out(finished[u], results[u])
+                if u == late or ring == 2 or d != ring // 2 - 1:
+                    arrived(done(u, h, k), sem4(u, h, k))
+                if u == late and h == 1:
+                    store_out(finished[u].at[rows_of(k)], results[u].at[rows_of(k)])
+        if u == late:
+            store_out(finished[u].at[rows_of(me1[1])], results[u].at[rows_of(me1[1])])
+        else:
+            store_out(finished[u], results[u])
 
     for d in range(1, groups):
         q = lax.rem(ch + d, groups)
@@ -539,27 +559,23 @@
     store_out(output_ref.at[pl.ds(0, half)], output_out.at[pl.ds(0, half)])
 
     second_sum(of_out)
+    cross(of_gate)
+    second_sum(late)
     second_gather(of_gate)
-    second_sum(late)
-    second_gather(of_out)
+    cross(of_out)
     arrived(product_recv, product_sem)
     output_ref[half:rows, :] = (
         block_in[ch, half:rows, :].astype(F32) + product_recv[...].astype(F32)
     ).astype(BF16)
     store_out(output_ref.at[pl.ds(half, half)], output_out.at[pl.ds(half, half)])
+    cross(late)
+    second_gather(of_out)
     first_gather(of_gate)
     second_gather(late)
     first_gather(of_out)
     first_gather(late)
-    for h in range(2):
-        for dx in range(1, xs):
-            x = lax.rem(my_x + dx, xs)
-            arrived(conv_x.at[h, x], conv_sem + h * xs + x)
-        tail = jnp.zeros((conv_rows, lanes), F32)
-        for x in range(xs):
-            tail = tail + conv_x[h, x].astype(F32)
-        for level in range(3):
-            grad_conv_ref[level, :, side(h)] = tail[4 * level : 4 * level + 4]
+    relay(of_gate)
+    relay(of_out)
     store_out(grad_conv_ref, grad_conv_out)
     finish(of_gate)
     finish(of_out)
@@ -656,8 +672,8 @@
             held(3, 2, ys, size + 16, width // 2),
             held(3, 2, ys, size + 16, width // 2),
             held(2, zs, 3 * part + 16, width // 2),
-            held(2, xs * zs, 3 * part + 16, width // 2),
-            held(2, xs, 16, width // 2),
+            held(2, zs, 3 * part + 16, width // 2),
+            held(2, xs, 3 * part + 16, width // 2),
             dma((SENDS,)),
             dma((RECEIVES,)),
             dma((32,)),

time: 117 us -> 115 us (0.983)
    pallas_call x1, Pallas kernels: 113 us -> 112 us  [local(): pl.pallas_call(functools.partial(block_kernel, sizes, groups), out_shape=...]
where the time goes in v6:
time: 115 us
  Pallas kernels  114 us (99%)
    pallas_call x1, Pallas kernels, local(): pl.pallas_call(functools.partial(block_kernel, sizes, groups), out_shape=...  112 us
    pallas_call x1, Pallas kernels, local(): pl.pallas_call(hand_over, out_shape=results, in_specs=[anywhere] * 5, out...  2.35 us

profile of v6, /device:TPU:6, one launch (start us, length us, event | category | flops | bytes accessed | tf_op | source)
XLA Modules:
  0.0 114.5 jit_solution(17609914477796671513)
XLA Ops:
  0.6 111.5 %shard_map.137 = (bf16[512,256]{1,0:T(8,128)(2,1)}, bf16[1024,256]{1,0:T(8,128)(2,1)}, bf16[1024,256]{1,0:T(8,128)(2,1)}, bf16[1024,256]{1,0:T(8,128)(2,1)}, f32[3,4,256]{2,1,0:T(4,128)}) custom-call(s32[1,512]{1,0:T(1,128)} %bitcast.5, bf16[512,256]{1,0:T(8,128)(2,1)} %hidden_in.1, bf16[4,256]{1,0:T(4,128)(2,1)} %embedding_in.1, bf16[1024,256]{1,0:T(8,128)(2,1)} %w_in_in.1, ...), custom_call_target="tpu_custom_call" | custom-call | tf_op jit(solution)/shard_map/pallas_call | solution.py:623
  112.2 2.4 %shard_map.138 = (bf16[512,256]{1,0:T(8,128)(2,1)}, bf16[1024,256]{1,0:T(8,128)(2,1)}, bf16[1024,256]{1,0:T(8,128)(2,1)}, bf16[1024,256]{1,0:T(8,128)(2,1)}, f32[3,4,256]{2,1,0:T(4,128)}) custom-call(bf16[512,256]{1,0:T(8,128)(2,1)} %get-tuple-element.10.refs_0_, bf16[1024,256]{1,0:T(8,128)(2,1)} %get-tuple-element.11.refs_1_, ...), custom_call_target="tpu_custom_call" | custom-call | tf_op jit(solution)/shard_map/pallas_call | solution.py:688

commit v7 on v6

--- a/solution.py
+++ b/solution.py
@@ -21,7 +21,7 @@
 
 
 def ring_sizes(count):
-    return {128: (2, 8, 8), 8: (2, 2, 2), 4: (1, 2, 2)}[count]
+    return {128: (2, 8, 8), 16: (1, 4, 4), 8: (2, 2, 2), 4: (1, 2, 2)}[count]
 
 
 def dot(a, b, contract):
@@ -36,7 +36,7 @@
     sizes, groups,
     tokens_in, hidden_in, embedding_in, w_in_in, w_gate_in, conv_w_in, order_in, gain_in, w_out_in, cot_in,
     output_out, grad_in_out, grad_gate_out, grad_out_out, grad_conv_out,
-    tokens_ref, hidden_ref, w_in_ref, w_gate_ref, conv_w_ref, order_ref, gain_ref, w_out_ref,
+    tokens_ref, hidden_ref, embedding_ref, w_in_ref, w_gate_ref, conv_w_ref, order_ref, gain_ref, w_out_ref,
     output_ref, grad_in_ref, grad_gate_ref, grad_out_ref, grad_conv_ref,
     block_in, embed, level0, level1, level2, level3, gate_pre, halo_send, halo_recv, halo_late,
     gated, both, permute, cot_near, cot_far, cot_mix, term_send, term_recv, term_cross, norm_mix, grad_split,
@@ -136,7 +136,7 @@
     loads = {}
     for name, src, dst in (
         ("tokens", tokens_in, tokens_ref),
-        ("embedding", embedding_in, embed.at[pl.ds(0, 4)]),
+        ("embedding", embedding_in, embedding_ref),
         ("hidden", hidden_in, hidden_ref),
         ("cot", cot_in.at[pl.ds(0, half)], cot_near),
         ("order", order_in, order_ref),
@@ -157,6 +157,7 @@
 
     for name in ("tokens", "embedding", "hidden"):
         loads[name].wait()
+    embed[0:4, :] = embedding_ref[...]
     hot = (lax.broadcasted_iota(jnp.int32, (16, rows), 0) == tokens_ref[...]).astype(F32).astype(BF16)
     looked_up = dot(hot, embed[...], (0, 0))
     block_in[ch] = (hidden_ref[...].astype(F32) + looked_up).astype(BF16)
@@ -628,6 +629,7 @@
         scratch_shapes=[
             held(1, rows, dtype=jnp.int32),
             held(rows, width),
+            held(4, width),
             held(full, width),
             held(full, width),
             held(3, 4, width, dtype=F32),

time: 115 us -> 115 us (level)
  no operation moved by 1% of the time
where the time goes in v7:
time: 115 us
  Pallas kernels  114 us (99%)
    pallas_call x1, Pallas kernels, local(): pl.pallas_call(functools.partial(block_kernel, sizes, groups), out_shape=...  112 us
    pallas_call x1, Pallas kernels, local(): pl.pallas_call(hand_over, out_shape=results, in_specs=[anywhere] * 5, out...  2.35 us

profile of v7, /device:TPU:6, one launch (start us, length us, event | category | flops | bytes accessed | tf_op | source)
XLA Modules:
  0.0 114.5 jit_solution(662223108830242087)
XLA Ops:
  0.6 111.5 %shard_map.137 = (bf16[512,256]{1,0:T(8,128)(2,1)}, bf16[1024,256]{1,0:T(8,128)(2,1)}, bf16[1024,256]{1,0:T(8,128)(2,1)}, bf16[1024,256]{1,0:T(8,128)(2,1)}, f32[3,4,256]{2,1,0:T(4,128)}) custom-call(s32[1,512]{1,0:T(1,128)} %bitcast.5, bf16[512,256]{1,0:T(8,128)(2,1)} %hidden_in.1, bf16[4,256]{1,0:T(4,128)(2,1)} %embedding_in.1, bf16[1024,256]{1,0:T(8,128)(2,1)} %w_in_in.1, ...), custom_call_target="tpu_custom_call" | custom-call | tf_op jit(solution)/shard_map/pallas_call | solution.py:624
  112.2 2.4 %shard_map.138 = (bf16[512,256]{1,0:T(8,128)(2,1)}, bf16[1024,256]{1,0:T(8,128)(2,1)}, bf16[1024,256]{1,0:T(8,128)(2,1)}, bf16[1024,256]{1,0:T(8,128)(2,1)}, f32[3,4,256]{2,1,0:T(4,128)}) custom-call(bf16[512,256]{1,0:T(8,128)(2,1)} %get-tuple-element.10.refs_0_, bf16[1024,256]{1,0:T(8,128)(2,1)} %get-tuple-element.11.refs_1_, ...), custom_call_target="tpu_custom_call" | custom-call | tf_op jit(solution)/shard_map/pallas_call | solution.py:690
